TPU v7x, 512 devices: a whole 4x8x8 slice. The times are simulated.
512 devices in a mesh: gx: 32 (over x, z), gy: 16 (over y, core).
Axes of the slice: x: 4, y: 8, z: 8, core: 2. Of those that a mesh axis runs over, the one named last changes fastest.
Arguments:
- features: bfloat16 [96, 2097152], P(None, ('gx', 'gy')), may hold values from -6 to 6
- kernel_map: int32 [27, 2097152], P(None, ('gx', 'gy')), may hold values from 0 to 13312, as said below
- send_rows: int32 [524288], P(('gx', 'gy')), may hold values from 0 to 4095
- conv_weight: bfloat16 [27, 96, 96], replicated, may hold values from -0.15625 to 0.15625
- conv_gain: float32 [96], replicated, may hold values from 0.5 to 1.5
- conv_bias: float32 [96], replicated, may hold values from -2 to 2
- down_weight: bfloat16 [8, 192, 96], replicated, may hold values from -0.3125 to 0.3125
- coarse_dest: int32 [512], P(('gx', 'gy')), may hold values from 0 to 3
Outputs:
- fine_out: bfloat16 [96, 2097152], P(None, ('gx', 'gy'))
- coarse_out: bfloat16 [192, 262144], P(None, ('gx', 'gy'))
Inputs may be any that keep to these rules, and one draw needn't show every extreme that they name: kernel_map[13, q] is q's own slot within its device where q is occupied and 13312 elsewhere; the value 4096 + 9 * 1024 means no input.
All inputs are finite; a program needn't handle non-finite values.
Results may differ from a plain program's by a relative error of at most 0.0095.
Values may be sent and summed in bfloat16 or wider, within the bound.
A program may use at most 64 MiB of HBM per device.

v0:
```python
import jax
import jax.numpy as jnp
from jax import lax
from jax.sharding import PartitionSpec as P


def padded(shard, sides, width):
    for axis, dim in sides:
        devices, length = (lax.axis_size(axis), shard.shape[dim])
        up = [(i, (i + 1) % devices) for i in range(devices - 1)]
        down = [(j, i) for i, j in up]
        last = lax.slice_in_dim(shard, length - width, length, axis=dim)
        leading = lax.slice_in_dim(shard, 0, width, axis=dim)
        before = lax.ppermute(last, axis, up)
        after = lax.ppermute(leading, axis, down)
        shard = jnp.concatenate([before, shard, after], axis=dim)
    return shard


def passed_along(shard, axis, by):
    devices = lax.axis_size(axis)
    pairs = [(i, i + by) for i in range(devices) if 0 <= i + by < devices]
    return lax.ppermute(shard, axis, pairs)


def route_blocks(dest, partial_value, block_count):
    one_hot = (dest[:, None] == jnp.arange(4 * block_count, dtype=jnp.int32)[None, :]).astype(
        jnp.float32
    )
    return jnp.einsum("bq,bov->qov", one_hot, partial_value, precision=lax.Precision.HIGHEST)


def shards(
    features, kernel_map, send_rows, conv_weight, conv_gain, conv_bias, down_weight, coarse_dest
):
    channels, slots_dev = features.shape
    boundary_len = send_rows.shape[0]
    offsets_count = kernel_map.shape[0]
    feature_rows = jnp.transpose(features)
    boundary = jnp.take(feature_rows, send_rows, axis=0)
    boundary = jnp.transpose(boundary).reshape(channels, 1, 1, boundary_len)
    beside_all = padded(boundary, (("gx", 1), ("gy", 2)), 1)
    around_rows = jnp.transpose(beside_all.reshape(channels, 9 * boundary_len))
    lookup_rows = jnp.concatenate([feature_rows, around_rows], axis=0)
    zeros_total = jnp.zeros((channels, slots_dev), jnp.float32)

    def add_offset(totals, offset):
        gathered = jnp.take(lookup_rows, kernel_map[offset], axis=0, mode="fill", fill_value=0)
        product = lax.dot_general(
            conv_weight[offset],
            gathered,
            (((1,), (1,)), ((), ())),
            preferred_element_type=jnp.float32,
        )
        return (totals + product, None)

    totals, _ = lax.scan(add_offset, zeros_total, jnp.arange(offsets_count, dtype=jnp.int32))
    active = (kernel_map[offsets_count // 2] < slots_dev).astype(jnp.float32)
    fine_out = (
        jax.nn.relu(totals * conv_gain[:, None] + conv_bias[:, None]) * active[None, :]
    ).astype(jnp.bfloat16)
    block_count = coarse_dest.shape[0]
    coarse_len = slots_dev // block_count // 8
    out_channels = down_weight.shape[1]
    planes = fine_out.reshape(channels, block_count, 8, coarse_len)
    partial_value = jnp.einsum(
        "pod,dbpv->bov", down_weight, planes, preferred_element_type=jnp.float32
    )
    routed = route_blocks(coarse_dest, partial_value, block_count)
    routed = routed.reshape(4, block_count, out_channels, coarse_len)
    from_x = passed_along(routed[1].astype(jnp.bfloat16), "gx", -1).astype(jnp.float32)
    from_y = passed_along(routed[2].astype(jnp.bfloat16), "gy", -1).astype(jnp.float32)
    corner_part = passed_along(routed[3].astype(jnp.bfloat16), "gx", -1).astype(jnp.float32)
    from_corner = passed_along(corner_part.astype(jnp.bfloat16), "gy", -1).astype(corner_part.dtype)
    summed = routed[0] + from_x + from_y + from_corner
    coarse_out = (
        jnp.transpose(summed, (1, 0, 2))
        .reshape(out_channels, block_count * coarse_len)
        .astype(jnp.bfloat16)
    )
    return (fine_out, coarse_out)


def solution(mesh):
    placed = (
        P(None, ("gx", "gy")),
        P(None, ("gx", "gy")),
        P(("gx", "gy")),
        P(),
        P(),
        P(),
        P(),
        P(("gx", "gy")),
    )
    return jax.shard_map(
        shards,
        mesh=mesh,
        in_specs=placed,
        out_specs=(P(None, ("gx", "gy")), P(None, ("gx", "gy"))),
        check_vma=False,
    )
```

profile of v0, /device:TPU:29, one launch (start us, length us, event | category | flops | bytes accessed | tf_op | source)
XLA Modules:
  0.0 672.6 jit_solution(17526937420969389404)
XLA Ops:
  7.0 4.0 collective-permute-start
  11.1 8.6 %collective-permute-start.1 = (bf16[96,1,1,1024]{0,3,2,1:T(8,128)(2,1)S(1)}, bf16[96,1,1,1024]{0,3,2,1:T(8,128)(2,1)S(1)}, u32[]{:S(2)}, u32[]{:S(2)}) collective-permute-start(bf16[96,1,1,1024]{0,3,2,1:T(8,128)(2,1)S(1)} %select_bitcast_fusion), channel_id=1, source_target_pairs={{16,0},{32,16},{48,32},{64,48},{80,64},{96,80},{112,96},{128,112},... | collective-permute-start | bytes 589832 | tf_op jit(solution)/shard_map/ppermute | solution.py:15
  25.0 5.9 collective-permute-start.2
  33.8 3.9 collective-permute-done.2
  38.1 5.2 collective-permute-done.3
  44.9 7.5 %pad_maximum_fusion = bf16[13312,96]{1,0:T(8,128)(2,1)S(1)} fusion(bf16[9216,96]{1,0:T(8,128)(2,1)S(1)} %bitcast.46, bf16[4096,96]{1,0:T(8,128)(2,1)S(1)} %bitcast.45), kind=kLoop, calls=%fused_computation.15 | loop fusion | flops 5111808 | bytes 5111808 | tf_op jit(solution)/shard_map/concatenate | solution.py:44
  52.4 597.8 %while.11 = (s32[]{:T(128)}, f32[96,4096]{1,0:T(8,128)}, s32[27]{0:T(128)S(1)}, bf16[27,96,96]{2,1,0:T(8,128)(2,1)}, s32[27,4096]{1,0:T(8,128)}, /*index=5*/bf16...) while((s32[]{:T(128)}, f32[96,4096]{1,0:T(8,128)}, s32[27]{0:T(128)S(1)}, ...), condition=%wide.region_1.2_spmd.clone, body=%wide.region_0.1_spmd.clone.sunk | while | flops 76718088 | bytes 5914781 | solution.py:57
  55.9 14.9 %gather_fusion = bf16[4096,96]{1,0:T(8,128)(2,1)} fusion(bf16[13312,96]{1,0:T(8,128)(2,1)S(1)} %get-tuple-element.139, s32[4096]{0:T(1024)S(1)} %broadcast_clamp_fusion.2), kind=kCustom, calls=%fused_computation.clone.clone.1 | custom fusion | bytes 1589248 | tf_op jit(solution)/shard_map/while/body/eval_jaxpr/jit(_take)/gather | solution.py:48
  77.6 14.9 %gather_fusion = bf16[4096,96]{1,0:T(8,128)(2,1)} fusion(bf16[13312,96]{1,0:T(8,128)(2,1)S(1)} %get-tuple-element.139, s32[4096]{0:T(1024)S(1)} %broadcast_clamp_fusion.2), kind=kCustom, calls=%fused_computation.clone.clone.1 | custom fusion | bytes 1589248 | tf_op jit(solution)/shard_map/while/body/eval_jaxpr/jit(_take)/gather | solution.py:48
  92.5 3.8 convolution_add_fusion.2
  99.7 14.9 %gather_fusion = bf16[4096,96]{1,0:T(8,128)(2,1)} fusion(bf16[13312,96]{1,0:T(8,128)(2,1)S(1)} %get-tuple-element.139, s32[4096]{0:T(1024)S(1)} %broadcast_clamp_fusion.2), kind=kCustom, calls=%fused_computation.clone.clone.1 | custom fusion | bytes 1589248 | tf_op jit(solution)/shard_map/while/body/eval_jaxpr/jit(_take)/gather | solution.py:48
  121.9 14.9 %gather_fusion = bf16[4096,96]{1,0:T(8,128)(2,1)} fusion(bf16[13312,96]{1,0:T(8,128)(2,1)S(1)} %get-tuple-element.139, s32[4096]{0:T(1024)S(1)} %broadcast_clamp_fusion.2), kind=kCustom, calls=%fused_computation.clone.clone.1 | custom fusion | bytes 1589248 | tf_op jit(solution)/shard_map/while/body/eval_jaxpr/jit(_take)/gather | solution.py:48
  136.8 3.8 convolution_add_fusion.2
  144.1 14.9 %gather_fusion = bf16[4096,96]{1,0:T(8,128)(2,1)} fusion(bf16[13312,96]{1,0:T(8,128)(2,1)S(1)} %get-tuple-element.139, s32[4096]{0:T(1024)S(1)} %broadcast_clamp_fusion.2), kind=kCustom, calls=%fused_computation.clone.clone.1 | custom fusion | bytes 1589248 | tf_op jit(solution)/shard_map/while/body/eval_jaxpr/jit(_take)/gather | solution.py:48
  166.2 14.9 %gather_fusion = bf16[4096,96]{1,0:T(8,128)(2,1)} fusion(bf16[13312,96]{1,0:T(8,128)(2,1)S(1)} %get-tuple-element.139, s32[4096]{0:T(1024)S(1)} %broadcast_clamp_fusion.2), kind=kCustom, calls=%fused_computation.clone.clone.1 | custom fusion | bytes 1589248 | tf_op jit(solution)/shard_map/while/body/eval_jaxpr/jit(_take)/gather | solution.py:48
  181.1 3.8 convolution_add_fusion.2
  188.4 14.9 %gather_fusion = bf16[4096,96]{1,0:T(8,128)(2,1)} fusion(bf16[13312,96]{1,0:T(8,128)(2,1)S(1)} %get-tuple-element.139, s32[4096]{0:T(1024)S(1)} %broadcast_clamp_fusion.2), kind=kCustom, calls=%fused_computation.clone.clone.1 | custom fusion | bytes 1589248 | tf_op jit(solution)/shard_map/while/body/eval_jaxpr/jit(_take)/gather | solution.py:48
  210.5 14.9 %gather_fusion = bf16[4096,96]{1,0:T(8,128)(2,1)} fusion(bf16[13312,96]{1,0:T(8,128)(2,1)S(1)} %get-tuple-element.139, s32[4096]{0:T(1024)S(1)} %broadcast_clamp_fusion.2), kind=kCustom, calls=%fused_computation.clone.clone.1 | custom fusion | bytes 1589248 | tf_op jit(solution)/shard_map/while/body/eval_jaxpr/jit(_take)/gather | solution.py:48
  232.7 14.9 %gather_fusion = bf16[4096,96]{1,0:T(8,128)(2,1)} fusion(bf16[13312,96]{1,0:T(8,128)(2,1)S(1)} %get-tuple-element.139, s32[4096]{0:T(1024)S(1)} %broadcast_clamp_fusion.2), kind=kCustom, calls=%fused_computation.clone.clone.1 | custom fusion | bytes 1589248 | tf_op jit(solution)/shard_map/while/body/eval_jaxpr/jit(_take)/gather | solution.py:48
  247.6 3.8 convolution_add_fusion.2
  254.8 14.9 %gather_fusion = bf16[4096,96]{1,0:T(8,128)(2,1)} fusion(bf16[13312,96]{1,0:T(8,128)(2,1)S(1)} %get-tuple-element.139, s32[4096]{0:T(1024)S(1)} %broadcast_clamp_fusion.2), kind=kCustom, calls=%fused_computation.clone.clone.1 | custom fusion | bytes 1589248 | tf_op jit(solution)/shard_map/while/body/eval_jaxpr/jit(_take)/gather | solution.py:48
  269.8 3.8 convolution_add_fusion.2
  277.0 14.9 %gather_fusion = bf16[4096,96]{1,0:T(8,128)(2,1)} fusion(bf16[13312,96]{1,0:T(8,128)(2,1)S(1)} %get-tuple-element.139, s32[4096]{0:T(1024)S(1)} %broadcast_clamp_fusion.2), kind=kCustom, calls=%fused_computation.clone.clone.1 | custom fusion | bytes 1589248 | tf_op jit(solution)/shard_map/while/body/eval_jaxpr/jit(_take)/gather | solution.py:48
  299.2 14.9 %gather_fusion = bf16[4096,96]{1,0:T(8,128)(2,1)} fusion(bf16[13312,96]{1,0:T(8,128)(2,1)S(1)} %get-tuple-element.139, s32[4096]{0:T(1024)S(1)} %broadcast_clamp_fusion.2), kind=kCustom, calls=%fused_computation.clone.clone.1 | custom fusion | bytes 1589248 | tf_op jit(solution)/shard_map/while/body/eval_jaxpr/jit(_take)/gather | solution.py:48
  314.1 3.8 convolution_add_fusion.2
  321.3 14.9 %gather_fusion = bf16[4096,96]{1,0:T(8,128)(2,1)} fusion(bf16[13312,96]{1,0:T(8,128)(2,1)S(1)} %get-tuple-element.139, s32[4096]{0:T(1024)S(1)} %broadcast_clamp_fusion.2), kind=kCustom, calls=%fused_computation.clone.clone.1 | custom fusion | bytes 1589248 | tf_op jit(solution)/shard_map/while/body/eval_jaxpr/jit(_take)/gather | solution.py:48
  343.5 14.9 %gather_fusion = bf16[4096,96]{1,0:T(8,128)(2,1)} fusion(bf16[13312,96]{1,0:T(8,128)(2,1)S(1)} %get-tuple-element.139, s32[4096]{0:T(1024)S(1)} %broadcast_clamp_fusion.2), kind=kCustom, calls=%fused_computation.clone.clone.1 | custom fusion | bytes 1589248 | tf_op jit(solution)/shard_map/while/body/eval_jaxpr/jit(_take)/gather | solution.py:48
  365.6 14.9 %gather_fusion = bf16[4096,96]{1,0:T(8,128)(2,1)} fusion(bf16[13312,96]{1,0:T(8,128)(2,1)S(1)} %get-tuple-element.139, s32[4096]{0:T(1024)S(1)} %broadcast_clamp_fusion.2), kind=kCustom, calls=%fused_computation.clone.clone.1 | custom fusion | bytes 1589248 | tf_op jit(solution)/shard_map/while/body/eval_jaxpr/jit(_take)/gather | solution.py:48
  380.6 3.8 convolution_add_fusion.2
  387.8 14.9 %gather_fusion = bf16[4096,96]{1,0:T(8,128)(2,1)} fusion(bf16[13312,96]{1,0:T(8,128)(2,1)S(1)} %get-tuple-element.139, s32[4096]{0:T(1024)S(1)} %broadcast_clamp_fusion.2), kind=kCustom, calls=%fused_computation.clone.clone.1 | custom fusion | bytes 1589248 | tf_op jit(solution)/shard_map/while/body/eval_jaxpr/jit(_take)/gather | solution.py:48
  402.7 3.8 convolution_add_fusion.2
  410.0 14.9 %gather_fusion = bf16[4096,96]{1,0:T(8,128)(2,1)} fusion(bf16[13312,96]{1,0:T(8,128)(2,1)S(1)} %get-tuple-element.139, s32[4096]{0:T(1024)S(1)} %broadcast_clamp_fusion.2), kind=kCustom, calls=%fused_computation.clone.clone.1 | custom fusion | bytes 1589248 | tf_op jit(solution)/shard_map/while/body/eval_jaxpr/jit(_take)/gather | solution.py:48
  432.1 14.9 %gather_fusion = bf16[4096,96]{1,0:T(8,128)(2,1)} fusion(bf16[13312,96]{1,0:T(8,128)(2,1)S(1)} %get-tuple-element.139, s32[4096]{0:T(1024)S(1)} %broadcast_clamp_fusion.2), kind=kCustom, calls=%fused_computation.clone.clone.1 | custom fusion | bytes 1589248 | tf_op jit(solution)/shard_map/while/body/eval_jaxpr/jit(_take)/gather | solution.py:48
  447.0 3.8 convolution_add_fusion.2
  454.3 14.9 %gather_fusion = bf16[4096,96]{1,0:T(8,128)(2,1)} fusion(bf16[13312,96]{1,0:T(8,128)(2,1)S(1)} %get-tuple-element.139, s32[4096]{0:T(1024)S(1)} %broadcast_clamp_fusion.2), kind=kCustom, calls=%fused_computation.clone.clone.1 | custom fusion | bytes 1589248 | tf_op jit(solution)/shard_map/while/body/eval_jaxpr/jit(_take)/gather | solution.py:48
  469.2 3.8 convolution_add_fusion.2
  476.4 14.9 %gather_fusion = bf16[4096,96]{1,0:T(8,128)(2,1)} fusion(bf16[13312,96]{1,0:T(8,128)(2,1)S(1)} %get-tuple-element.139, s32[4096]{0:T(1024)S(1)} %broadcast_clamp_fusion.2), kind=kCustom, calls=%fused_computation.clone.clone.1 | custom fusion | bytes 1589248 | tf_op jit(solution)/shard_map/while/body/eval_jaxpr/jit(_take)/gather | solution.py:48
  498.6 14.9 %gather_fusion = bf16[4096,96]{1,0:T(8,128)(2,1)} fusion(bf16[13312,96]{1,0:T(8,128)(2,1)S(1)} %get-tuple-element.139, s32[4096]{0:T(1024)S(1)} %broadcast_clamp_fusion.2), kind=kCustom, calls=%fused_computation.clone.clone.1 | custom fusion | bytes 1589248 | tf_op jit(solution)/shard_map/while/body/eval_jaxpr/jit(_take)/gather | solution.py:48
  513.5 3.8 convolution_add_fusion.2
  520.8 14.9 %gather_fusion = bf16[4096,96]{1,0:T(8,128)(2,1)} fusion(bf16[13312,96]{1,0:T(8,128)(2,1)S(1)} %get-tuple-element.139, s32[4096]{0:T(1024)S(1)} %broadcast_clamp_fusion.2), kind=kCustom, calls=%fused_computation.clone.clone.1 | custom fusion | bytes 1589248 | tf_op jit(solution)/shard_map/while/body/eval_jaxpr/jit(_take)/gather | solution.py:48
  542.9 14.9 %gather_fusion = bf16[4096,96]{1,0:T(8,128)(2,1)} fusion(bf16[13312,96]{1,0:T(8,128)(2,1)S(1)} %get-tuple-element.139, s32[4096]{0:T(1024)S(1)} %broadcast_clamp_fusion.2), kind=kCustom, calls=%fused_computation.clone.clone.1 | custom fusion | bytes 1589248 | tf_op jit(solution)/shard_map/while/body/eval_jaxpr/jit(_take)/gather | solution.py:48
  557.8 3.8 convolution_add_fusion.2
  565.1 14.9 %gather_fusion = bf16[4096,96]{1,0:T(8,128)(2,1)} fusion(bf16[13312,96]{1,0:T(8,128)(2,1)S(1)} %get-tuple-element.139, s32[4096]{0:T(1024)S(1)} %broadcast_clamp_fusion.2), kind=kCustom, calls=%fused_computation.clone.clone.1 | custom fusion | bytes 1589248 | tf_op jit(solution)/shard_map/while/body/eval_jaxpr/jit(_take)/gather | solution.py:48
  587.2 14.9 %gather_fusion = bf16[4096,96]{1,0:T(8,128)(2,1)} fusion(bf16[13312,96]{1,0:T(8,128)(2,1)S(1)} %get-tuple-element.139, s32[4096]{0:T(1024)S(1)} %broadcast_clamp_fusion.2), kind=kCustom, calls=%fused_computation.clone.clone.1 | custom fusion | bytes 1589248 | tf_op jit(solution)/shard_map/while/body/eval_jaxpr/jit(_take)/gather | solution.py:48
  609.4 14.9 %gather_fusion = bf16[4096,96]{1,0:T(8,128)(2,1)} fusion(bf16[13312,96]{1,0:T(8,128)(2,1)S(1)} %get-tuple-element.139, s32[4096]{0:T(1024)S(1)} %broadcast_clamp_fusion.2), kind=kCustom, calls=%fused_computation.clone.clone.1 | custom fusion | bytes 1589248 | tf_op jit(solution)/shard_map/while/body/eval_jaxpr/jit(_take)/gather | solution.py:48
  624.3 3.8 convolution_add_fusion.2
  631.5 14.9 %gather_fusion = bf16[4096,96]{1,0:T(8,128)(2,1)} fusion(bf16[13312,96]{1,0:T(8,128)(2,1)S(1)} %get-tuple-element.139, s32[4096]{0:T(1024)S(1)} %broadcast_clamp_fusion.2), kind=kCustom, calls=%fused_computation.clone.clone.1 | custom fusion | bytes 1589248 | tf_op jit(solution)/shard_map/while/body/eval_jaxpr/jit(_take)/gather | solution.py:48
  653.3 6.2 collective-permute-start.6
  (169 shorter events, 125.3 us)
Async XLA Ops:
  3.6 17.1 %copy-start = (bf16[96,4096]{0,1:T(8,128)(2,1)}, bf16[96,4096]{0,1:T(8,128)(2,1)S(1)}, u32[]{:S(2)}) copy-start(bf16[96,4096]{0,1:T(8,128)(2,1)S(1)} %copy.14) | copy-start | bytes 2359300
  3.6 16.0 %copy-start.4 = (bf16[8,192,96]{2,1,0:T(8,128)(2,1)S(1)}, bf16[8,192,96]{2,1,0:T(8,128)(2,1)}, u32[]{:S(2)}) copy-start(bf16[8,192,96]{2,1,0:T(8,128)(2,1)} %param.16) | copy-start | bytes 884740
  7.0 16.7 %collective-permute-start = (bf16[96,1,1,1024]{0,3,2,1:T(8,128)(2,1)S(1)}, bf16[96,1,1,1024]{0,3,2,1:T(8,128)(2,1)S(1)}, u32[]{:S(2)}, u32[]{:S(2)}) collective-permute-start(bf16[96,1,1,1024]{0,3,2,1:T(8,128)(2,1)S(1)} %select_bitcast_fusion), channel_id=1, source_target_pairs={{0,16},{16,32},{32,48},{48,64},{64,80},{80,96},{96,112},{112,128},... | collective-permute-start | bytes 589832 | tf_op jit(solution)/shard_map/ppermute | solution.py:14
  11.1 13.5 %collective-permute-start.1 = (bf16[96,1,1,1024]{0,3,2,1:T(8,128)(2,1)S(1)}, bf16[96,1,1,1024]{0,3,2,1:T(8,128)(2,1)S(1)}, u32[]{:S(2)}, u32[]{:S(2)}) collective-permute-start(bf16[96,1,1,1024]{0,3,2,1:T(8,128)(2,1)S(1)} %select_bitcast_fusion), channel_id=1, source_target_pairs={{16,0},{32,16},{48,32},{64,48},{80,64},{96,80},{112,96},{128,112},... | collective-permute-start | bytes 589832 | tf_op jit(solution)/shard_map/ppermute | solution.py:15
  25.0 12.7 %collective-permute-start.2 = (bf16[96,3,1,1024]{3,0,2,1:T(8,128)(2,1)S(1)}, bf16[96,3,1,1024]{3,0,2,1:T(8,128)(2,1)S(1)}, u32[]{:S(2)}, u32[]{:S(2)}) collective-permute-start(bf16[96,3,1,1024]{3,0,2,1:T(8,128)(2,1)S(1)} %copy.15), channel_id=1, source_target_pairs={{0,1},{1,2},{2,3},{3,4},{4,5},{5,6},{6,7},{7,8},{8,9},{9,10},{10,1... | collective-permute-start | bytes 1769480 | tf_op jit(solution)/shard_map/ppermute | solution.py:14
  30.9 12.4 %collective-permute-start.3 = (bf16[96,3,1,1024]{3,0,2,1:T(8,128)(2,1)S(1)}, bf16[96,3,1,1024]{3,0,2,1:T(8,128)(2,1)S(1)}, u32[]{:S(2)}, u32[]{:S(2)}) collective-permute-start(bf16[96,3,1,1024]{3,0,2,1:T(8,128)(2,1)S(1)} %copy.15), channel_id=1, source_target_pairs={{1,0},{2,1},{3,2},{4,3},{5,4},{6,5},{7,6},{8,7},{9,8},{10,9},{11,1... | collective-permute-start | bytes 1769480 | tf_op jit(solution)/shard_map/ppermute | solution.py:15
  43.7 1.2 copy-start.1
  52.4 597.8 %copy-start.5 = (f32[96]{0:T(128)S(1)}, f32[96]{0:T(128)}, u32[]{:S(2)}) copy-start(f32[96]{0:T(128)} %param.15) | copy-start | bytes 1156
  52.4 597.8 %copy-start.6 = (f32[96]{0:T(128)S(1)}, f32[96]{0:T(128)}, u32[]{:S(2)}) copy-start(f32[96]{0:T(128)} %param.14) | copy-start | bytes 1156
  650.2 2.1 copy-start.3
  652.0 0.9 copy-start.2
  652.0 0.9 copy-start.7
  653.3 10.1 %collective-permute-start.6 = (bf16[1,192,512]{2,1,0:T(8,128)(2,1)S(1)}, bf16[1,192,512]{2,1,0:T(8,128)(2,1)S(1)}, u32[]{:S(2)}, u32[]{:S(2)}) collective-permute-start(bf16[1,192,512]{2,1,0:T(8,128)(2,1)S(1)} %get-tuple-element.71), channel_id=1, source_target_pairs={{16,0},{32,16},{48,32},{64,48},{80,64},{96,80},{112,96},{128,112},... | collective-permute-start | bytes 589832 | tf_op jit(solution)/shard_map/ppermute | solution.py:23
  659.5 6.4 collective-permute-start.4
  661.5 8.2 %collective-permute-start.5 = (bf16[1,192,512]{2,1,0:T(8,128)(2,1)S(1)}, bf16[1,192,512]{2,1,0:T(8,128)(2,1)S(1)}, u32[]{:S(2)}, u32[]{:S(2)}) collective-permute-start(bf16[1,192,512]{2,1,0:T(8,128)(2,1)S(1)} %get-tuple-element.72), channel_id=1, source_target_pairs={{1,0},{2,1},{3,2},{4,3},{5,4},{6,5},{7,6},{8,7},{9,8},{10,9},{11,1... | collective-permute-start | bytes 589832 | tf_op jit(solution)/shard_map/ppermute | solution.py:23
  663.4 8.4 %collective-permute-start.7 = (bf16[1,192,512]{2,1,0:T(8,128)(2,1)S(1)}, bf16[1,192,512]{2,1,0:T(8,128)(2,1)S(1)}, u32[]{:S(2)}, u32[]{:S(2)}) collective-permute-start(bf16[1,192,512]{2,1,0:T(8,128)(2,1)S(1)} %collective-permute-done.6), channel_id=1, source_target_pairs={{1,0},{2,1},{3,2},{4,3},{5,4},{6,5},{7,6},{8,7},{9,8},{10,9},{11,1... | collective-permute-start | bytes 589832 | tf_op jit(solution)/shard_map/ppermute | solution.py:23
where the time goes:
time: 675 us; the launch traced here: 673 us
  local copies, waits for them, and re-layouts  426 us (63%)
  matrix products  101 us (15%)
  loops' own time  53 us (8%)
  other arithmetic  40 us (6%)
  starting transfers between devices  32.3 us (5%)
  waiting for transfers between devices  18.2 us (3%)
    gather x27, local copies, waits for them, and re-layouts, add_offset(): jnp.take(lookup_rows, kernel_map[offset], axis=0, mode='fill', fill_value=0)  403 us
    dot_general x27, matrix products, add_offset(): lax.dot_general(conv_weight[offset], gathered, (((1,), (1,)), ((), ())),...  101 us
    another operation x1, loops' own time, shards(): lax.scan(add_offset, zeros_total, jnp.arange(offsets_count, dtype=jnp.int...  53 us
    select_n x27, other arithmetic, add_offset(): jnp.take(lookup_rows, kernel_map[offset], axis=0, mode='fill', fill_value=0)  25.3 us
    dynamic_slice x27, local copies, waits for them, and re-layouts, shards(): lax.scan(add_offset, zeros_total, jnp.arange(offsets_count, dtype=jnp.int...  15.7 us
  transfers between devices with their start and end apart: 8, of which 7 were waited for; matrix products, arithmetic and copies ran while one was open for 0% of the time, Pallas kernels for 0%

commit v1 on v0

v1 whole, which is shorter than its diff:
```python
import jax
import jax.numpy as jnp
from jax import lax
from jax.experimental import pallas as pl
from jax.experimental.pallas import tpu as pltpu
from jax.sharding import PartitionSpec as P

F32 = jnp.float32
BF16 = jnp.bfloat16
LANES = 128
QC = 512


def padded(shard, sides, width):
    for axis, dim in sides:
        devices, length = (lax.axis_size(axis), shard.shape[dim])
        up = [(i, (i + 1) % devices) for i in range(devices - 1)]
        down = [(j, i) for i, j in up]
        last = lax.slice_in_dim(shard, length - width, length, axis=dim)
        leading = lax.slice_in_dim(shard, 0, width, axis=dim)
        before = lax.ppermute(last, axis, up)
        after = lax.ppermute(leading, axis, down)
        shard = jnp.concatenate([before, shard, after], axis=dim)
    return shard


def passed_along(shard, axis, by):
    devices = lax.axis_size(axis)
    pairs = [(i, i + by) for i in range(devices) if 0 <= i + by < devices]
    return lax.ppermute(shard, axis, pairs)


def dot_nt(a, b):
    return lax.dot_general(a, b, (((1,), (1,)), ((), ())), preferred_element_type=F32)


def conv_kernel(
    map_ref, feat_ref, halo_ref, w_ref, gain_ref, bias_ref, down_ref,
    fine_ref, part_ref,
    idx_a, idx_b, tiles, table, wpair, acc, sems, ga0, ga1, gb0, gb1,
):
    channels, slots = feat_ref.shape
    halo_len = halo_ref.shape[1]
    koff = map_ref.shape[0]
    centre = koff // 2
    others = [k for k in range(koff) if k != centre]
    pairs = len(others) // 2
    blocks = slots // QC
    total = blocks * pairs
    lane_tiles = QC // LANES
    idx = (idx_a, idx_b)
    rows = ((ga0, ga1), (gb0, gb1))

    wpair[...] = jnp.zeros_like(wpair)
    for n, k in enumerate(others):
        wpair[n // 2, :, pl.ds((n % 2) * LANES, channels)] = w_ref[k]

    for b in range(blocks):
        for j in range(pairs):
            for h in range(2):
                for t in range(lane_tiles):
                    tiles[b * pairs + j, pl.ds(h * lane_tiles + t, 1), :] = map_ref[
                        pl.ds(others[2 * j + h], 1), pl.ds(b * QC + t * LANES, LANES)
                    ]

    step = 256
    eye = (
        lax.broadcasted_iota(jnp.int32, (step, step), 0)
        == lax.broadcasted_iota(jnp.int32, (step, step), 1)
    ).astype(BF16)
    pad = jnp.zeros((LANES - channels, step), BF16)

    def transpose_in(src, base, count):
        def one(i, _):
            c0 = pl.multiple_of(i * step, step)
            x = jnp.concatenate([src[:, pl.ds(c0, step)], pad], axis=0)
            table[pl.ds(pl.multiple_of(base + c0, step), step), :] = dot_nt(eye, x)
            return 0

        lax.fori_loop(0, count // step, one, 0)

    transpose_in(feat_ref, 0, slots)
    transpose_in(halo_ref, slots, halo_len)
    table[pl.ds(slots + halo_len, 8), :] = jnp.zeros((8, LANES), F32)

    def fetch(t, s):
        return pltpu.make_async_copy(tiles.at[t], idx[s], sems.at[s])

    def gather(s):
        for h in range(2):
            for r in range(QC):
                at = idx[s][h * lane_tiles + r // LANES, r % LANES]
                rows[s][h][pl.ds(r, 1), :] = table[pl.ds(at, 1), :]

    def multiply(t, s):
        j = lax.rem(t, pairs)
        g = jnp.concatenate([rows[s][0][...], rows[s][1][...]], axis=1).astype(BF16)
        keep = jnp.where(j == 0, 0.0, 1.0)
        acc[...] = acc[...] * keep + dot_nt(wpair[j], g)

    def finish(t):
        b = lax.div(t, pairs)

        @pl.when(t - b * pairs == pairs - 1)
        def _():
            cols = pl.ds(pl.multiple_of(b * QC, QC), QC)
            conv = acc[...] + jnp.dot(
                w_ref[centre], feat_ref[:, cols], preferred_element_type=F32
            )
            active = (map_ref[centre : centre + 1, cols] < slots).astype(F32)
            fine = jnp.maximum(conv * gain_ref[...] + bias_ref[...], 0.0) * active
            fine = fine.astype(BF16)
            fine_ref[:, cols] = fine
            prior = jnp.where(b == 0, 0.0, 1.0)
            part_ref[...] = part_ref[...] * prior + jnp.dot(
                down_ref[b], fine, preferred_element_type=F32
            )

    acc[...] = jnp.zeros_like(acc)
    part_ref[...] = jnp.zeros_like(part_ref)
    fetch(0, 0).start()
    fetch(1, 1).start()
    fetch(0, 0).wait()
    gather(0)
    fetch(2, 0).start()

    def body(i, _):
        for s in (1, 0):
            t = 2 * i + (1 if s == 1 else 2)
            fetch(t, s).wait()
            multiply(t - 1, 1 - s)
            gather(s)
            fetch(jnp.minimum(t + 2, total - 1), s).start()
            finish(t - 1)
        return 0

    lax.fori_loop(0, (total - 2) // 2, body, 0)
    fetch(total - 1, 1).wait()
    multiply(total - 2, 0)
    gather(1)
    finish(total - 2)
    multiply(total - 1, 1)
    finish(total - 1)
    fetch(total - 1, 0).wait()


def conv_call(kernel_map, features, halo, conv_weight, gain, bias, down_weight):
    channels, slots = features.shape
    koff = kernel_map.shape[0]
    pairs = koff // 2
    total = slots // QC * pairs
    out_channels = down_weight.shape[1]
    vmem = pl.BlockSpec(memory_space=pltpu.VMEM)
    return pl.pallas_call(
        conv_kernel,
        in_specs=[vmem] * 7,
        out_specs=[vmem] * 2,
        out_shape=[
            jax.ShapeDtypeStruct((channels, slots), BF16),
            jax.ShapeDtypeStruct((out_channels, slots // 8), F32),
        ],
        scratch_shapes=[
            pltpu.SMEM((8, LANES), jnp.int32),
            pltpu.SMEM((8, LANES), jnp.int32),
            pltpu.VMEM((total, 8, LANES), jnp.int32),
            pltpu.VMEM((slots + halo.shape[1] + 8, LANES), F32),
            pltpu.VMEM((pairs, channels, 2 * LANES), BF16),
            pltpu.VMEM((channels, QC), F32),
            pltpu.SemaphoreType.DMA((2,)),
        ]
        + [pltpu.VMEM((QC, LANES), F32)] * 4,
        compiler_params=pltpu.CompilerParams(vmem_limit_bytes=48 * 2**20),
        name="conv",
    )(kernel_map, features, halo, conv_weight, gain, bias, down_weight)


def shards(
    features, kernel_map, send_rows, conv_weight, conv_gain, conv_bias, down_weight, coarse_dest
):
    channels, slots_dev = features.shape
    boundary_len = send_rows.shape[0]
    feature_rows = jnp.transpose(features)
    boundary = jnp.take(feature_rows, send_rows, axis=0)
    boundary = jnp.transpose(boundary).reshape(channels, 1, 1, boundary_len)
    halo = padded(boundary, (("gx", 1), ("gy", 2)), 1).reshape(channels, 9 * boundary_len)
    fine_out, partial = conv_call(
        kernel_map, features, halo, conv_weight, conv_gain[:, None], conv_bias[:, None], down_weight
    )
    dest = coarse_dest[0]
    routed = [jnp.where(dest == c, partial, 0.0) for c in range(4)]
    from_x = passed_along(routed[1].astype(BF16), "gx", -1).astype(F32)
    from_y = passed_along(routed[2].astype(BF16), "gy", -1).astype(F32)
    corner = passed_along(routed[3].astype(BF16), "gx", -1)
    from_corner = passed_along(corner, "gy", -1).astype(F32)
    coarse_out = (routed[0] + from_x + from_y + from_corner).astype(BF16)
    return (fine_out, coarse_out)


def solution(mesh):
    placed = (
        P(None, ("gx", "gy")),
        P(None, ("gx", "gy")),
        P(("gx", "gy")),
        P(),
        P(),
        P(),
        P(),
        P(("gx", "gy")),
    )
    return jax.shard_map(
        shards,
        mesh=mesh,
        in_specs=placed,
        out_specs=(P(None, ("gx", "gy")), P(None, ("gx", "gy"))),
        check_vma=False,
    )
```

time: 675 us -> 158 us (0.23)
  the two profiles are of different devices: /device:TPU:29 before, /device:TPU:31 now
where the time goes in v1:
time: 158 us
  Pallas kernels  87.5 us (55%)
  starting transfers between devices  32.6 us (21%)
  waiting for transfers between devices  19.5 us (12%)
  local copies, waits for them, and re-layouts  12.1 us (8%)
  other arithmetic  4.49 us (3%)
    pallas_call x1, Pallas kernels, conv_call(): pl.pallas_call(conv_kernel, in_specs=[vmem] * 7, out_specs=[vmem] * 2, ou...  87.5 us
    ppermute x4, starting transfers between devices, passed_along(): return lax.ppermute(shard, axis, pairs)  12 us
    ppermute x2, starting transfers between devices, padded(): after = lax.ppermute(leading, axis, down)  10.8 us
    ppermute x2, starting transfers between devices, padded(): before = lax.ppermute(last, axis, up)  9.85 us
    ppermute x2, waiting for transfers between devices, padded(): before = lax.ppermute(last, axis, up)  8.08 us
    ppermute x4, waiting for transfers between devices, passed_along(): return lax.ppermute(shard, axis, pairs)  6.44 us
    ppermute x2, waiting for transfers between devices, padded(): after = lax.ppermute(leading, axis, down)  5.03 us
    unnamed x13, local copies, waits for them, and re-layouts  3.62 us
  transfers between devices with their start and end apart: 8, of which 7 were waited for; matrix products, arithmetic and copies ran while one was open for 1% of the time, Pallas kernels for 0%

profile of v1, /device:TPU:31, one launch (start us, length us, event | category | flops | bytes accessed | tf_op | source)
XLA Modules:
  0.0 157.7 jit_solution(9588484753731305492)
XLA Ops:
  0.6 0.7 fusion
  1.3 0.7 compare_and_fusion
  2.0 1.6 copy.18
  3.6 0.0 copy-start.4
  3.6 0.0 copy-start.5
  3.6 3.2 %gather_fusion = bf16[1024,96]{1,0:T(8,128)(2,1)S(1)} fusion(bf16[4096,96]{1,0:T(8,128)(2,1)S(1)} %bitcast.12, s32[1024]{0:T(1024)S(1)} %fusion), kind=kCustom, calls=%fused_computation | custom fusion | bytes 397312 | tf_op jit(solution)/shard_map/jit(_take)/gather | solution.py:183
  6.8 0.2 select_bitcast_fusion
  7.1 4.0 %collective-permute-start = (bf16[96,1,1,1024]{0,3,2,1:T(8,128)(2,1)S(1)}, bf16[96,1,1,1024]{0,3,2,1:T(8,128)(2,1)S(1)}, u32[]{:S(2)}, u32[]{:S(2)}) collective-permute-start(bf16[96,1,1,1024]{0,3,2,1:T(8,128)(2,1)S(1)} %select_bitcast_fusion), channel_id=1, source_target_pairs={{0,16},{16,32},{32,48},{48,64},{64,80},{80,96},{96,112},{112,128},... | collective-permute-start | bytes 589832 | tf_op jit(solution)/shard_map/ppermute | solution.py:21
  11.1 8.9 %collective-permute-start.1 = (bf16[96,1,1,1024]{0,3,2,1:T(8,128)(2,1)S(1)}, bf16[96,1,1,1024]{0,3,2,1:T(8,128)(2,1)S(1)}, u32[]{:S(2)}, u32[]{:S(2)}) collective-permute-start(bf16[96,1,1,1024]{0,3,2,1:T(8,128)(2,1)S(1)} %select_bitcast_fusion), channel_id=1, source_target_pairs={{16,0},{32,16},{48,32},{64,48},{80,64},{96,80},{112,96},{128,112},... | collective-permute-start | bytes 589832 | tf_op jit(solution)/shard_map/ppermute | solution.py:22
  19.9 4.1 %collective-permute-done = bf16[96,1,1,1024]{0,3,2,1:T(8,128)(2,1)S(1)} collective-permute-done((bf16[96,1,1,1024]{0,3,2,1:T(8,128)(2,1)S(1)}, bf16[96,1,1,1024]{0,3,2,1:T(8,128)(2,1)S(1)}, u32[]{:S(2)}, u32[]{:S(2)}) %collective-permute-start) | collective-permute-done | bytes 196640 | tf_op jit(solution)/shard_map/ppermute | solution.py:21
  24.0 0.9 collective-permute-done.1
  24.9 0.2 pad_maximum_fusion.1
  25.1 0.3 copy.19
  25.3 5.8 %collective-permute-start.2 = (bf16[96,3,1,1024]{3,0,2,1:T(8,128)(2,1)S(1)}, bf16[96,3,1,1024]{3,0,2,1:T(8,128)(2,1)}, u32[]{:S(2)}, u32[]{:S(2)}) collective-permute-start(bf16[96,3,1,1024]{3,0,2,1:T(8,128)(2,1)S(1)} %copy.19), channel_id=1, source_target_pairs={{0,1},{1,2},{2,3},{3,4},{4,5},{5,6},{6,7},{7,8},{8,9},{9,10},{10,1... | collective-permute-start | bytes 1769480 | tf_op jit(solution)/shard_map/ppermute | solution.py:21
  31.2 1.9 %collective-permute-start.3 = (bf16[96,3,1,1024]{3,0,2,1:T(8,128)(2,1)S(1)}, bf16[96,3,1,1024]{3,0,2,1:T(8,128)(2,1)S(1)}, u32[]{:S(2)}, u32[]{:S(2)}) collective-permute-start(bf16[96,3,1,1024]{3,0,2,1:T(8,128)(2,1)S(1)} %copy.19), channel_id=1, source_target_pairs={{1,0},{2,1},{3,2},{4,3},{5,4},{6,5},{7,6},{8,7},{9,8},{10,9},{11,1... | collective-permute-start | bytes 1769480 | tf_op jit(solution)/shard_map/ppermute | solution.py:22
  33.1 0.0 copy-done.4
  33.1 0.1 copy.24.gain_ref
  33.2 0.0 copy-done.5
  33.2 0.1 copy.25.bias_ref
  34.0 4.0 %collective-permute-done.2 = bf16[96,3,1,1024]{3,0,2,1:T(8,128)(2,1)} collective-permute-done((bf16[96,3,1,1024]{3,0,2,1:T(8,128)(2,1)S(1)}, bf16[96,3,1,1024]{3,0,2,1:T(8,128)(2,1)}, u32[]{:S(2)}, u32[]{:S(2)}) %collective-permute-start.2) | collective-permute-done | bytes 589856 | tf_op jit(solution)/shard_map/ppermute | solution.py:21
  38.0 1.4 copy.21
  39.4 4.2 %collective-permute-done.3 = bf16[96,3,1,1024]{3,0,2,1:T(8,128)(2,1)S(1)} collective-permute-done((bf16[96,3,1,1024]{3,0,2,1:T(8,128)(2,1)S(1)}, bf16[96,3,1,1024]{3,0,2,1:T(8,128)(2,1)S(1)}, u32[]{:S(2)}, u32[]{:S(2)}) %collective-permute-start.3) | collective-permute-done | bytes 589856 | tf_op jit(solution)/shard_map/ppermute | solution.py:22
  43.6 0.4 copy.22
  44.0 1.8 %pad_maximum_fusion = bf16[96,3,3,1024]{0,3,2,1:T(8,128)(2,1)} fusion(bf16[96,3,1,1024]{0,3,2,1:T(8,128)(2,1)S(1)} %copy.22, bf16[96,1,1,1024]{0,3,2,1:T(8,128)(2,1)S(1)} %collective-permute-done.1, bf16[96,1,1,1024]{0,3,2,1:T(8,128)(2,1)S(1)} %select_bitcast_fusion, bf16[96,1,1,1024]{0,3,2,1:T(8,128)(2,1)S(1)} %collective-permute-done, ...), kind=kLoop, calls=%fused_computation.1 | loop fusion | flops 3538944 | bytes 3538944 | tf_op jit(solution)/shard_map/concatenate | solution.py:23
  45.8 0.0 copy-start
  45.8 0.0 copy-start.1
  45.8 2.9 %copy.26.halo_ref = bf16[96,9216]{1,0:T(8,128)(2,1)S(1)} copy(bf16[96,9216]{0,1:T(8,128)(2,1)} %bitcast.13) | data formatting | bytes 3538944 | tf_op jit(solution)/shard_map/reshape | solution.py:185
  48.8 0.0 copy-done
  48.8 0.0 copy-done.1
  48.8 0.0 copy-start.2
  48.8 1.0 copy-done.2
  49.8 0.0 copy-start.3
  49.8 1.0 copy-done.3
  50.8 87.5 %conv.1 = (bf16[96,4096]{1,0:T(8,128)(2,1)}, f32[192,512]{1,0:T(8,128)S(1)}) custom-call(s32[27,4096]{1,0:T(8,128)S(1)} %copy-done.2, bf16[96,4096]{1,0:T(8,128)(2,1)S(1)} %copy-done, bf16[96,9216]{1,0:T(8,128)(2,1)S(1)} %copy.26.halo_ref, bf16[27,96,96]{2,1,0:T(8,128)(2,1)S(1)} %copy-done.1, f32[96,1]{1,0:T(8,128)S(1)} %copy.24.gain_ref, ...), custom_call_target="tpu_custom_call" | custom-call | tf_op jit(solution)/shard_map/conv/pallas_call | solution.py:154
  138.4 0.1 select_convert_fusion.2
  138.5 6.2 %collective-permute-start.6 = (bf16[192,512]{1,0:T(8,128)(2,1)S(1)}, bf16[192,512]{1,0:T(8,128)(2,1)S(1)}, u32[]{:S(2)}, u32[]{:S(2)}) collective-permute-start(bf16[192,512]{1,0:T(8,128)(2,1)S(1)} %get-tuple-element.7), channel_id=1, source_target_pairs={{16,0},{32,16},{48,32},{64,48},{80,64},{96,80},{112,96},{128,112},... | collective-permute-start | bytes 589832 | tf_op jit(solution)/shard_map/ppermute | solution.py:30
  144.7 1.9 %collective-permute-start.4 = (bf16[192,512]{1,0:T(8,128)(2,1)S(1)}, bf16[192,512]{1,0:T(8,128)(2,1)S(1)}, u32[]{:S(2)}, u32[]{:S(2)}) collective-permute-start(bf16[192,512]{1,0:T(8,128)(2,1)S(1)} %get-tuple-element.6), channel_id=1, source_target_pairs={{16,0},{32,16},{48,32},{64,48},{80,64},{96,80},{112,96},{128,112},... | collective-permute-start | bytes 589832 | tf_op jit(solution)/shard_map/ppermute | solution.py:30
  146.6 1.9 %collective-permute-start.5 = (bf16[192,512]{1,0:T(8,128)(2,1)S(1)}, bf16[192,512]{1,0:T(8,128)(2,1)S(1)}, u32[]{:S(2)}, u32[]{:S(2)}) collective-permute-start(bf16[192,512]{1,0:T(8,128)(2,1)S(1)} %get-tuple-element.8), channel_id=1, source_target_pairs={{1,0},{2,1},{3,2},{4,3},{5,4},{6,5},{7,6},{8,7},{9,8},{10,9},{11,1... | collective-permute-start | bytes 589832 | tf_op jit(solution)/shard_map/ppermute | solution.py:30
  148.5 0.0 collective-permute-done.6
  148.6 1.9 %collective-permute-start.7 = (bf16[192,512]{1,0:T(8,128)(2,1)S(1)}, bf16[192,512]{1,0:T(8,128)(2,1)S(1)}, u32[]{:S(2)}, u32[]{:S(2)}) collective-permute-start(bf16[192,512]{1,0:T(8,128)(2,1)S(1)} %collective-permute-done.6), channel_id=1, source_target_pairs={{1,0},{2,1},{3,2},{4,3},{5,4},{6,5},{7,6},{8,7},{9,8},{10,9},{11,1... | collective-permute-start | bytes 589832 | tf_op jit(solution)/shard_map/ppermute | solution.py:30
  150.5 0.6 collective-permute-done.4
  151.1 3.7 %collective-permute-done.5 = bf16[192,512]{1,0:T(8,128)(2,1)S(1)} collective-permute-done((bf16[192,512]{1,0:T(8,128)(2,1)S(1)}, bf16[192,512]{1,0:T(8,128)(2,1)S(1)}, u32[]{:S(2)}, u32[]{:S(2)}) %collective-permute-start.5) | collective-permute-done | bytes 196640 | tf_op jit(solution)/shard_map/ppermute | solution.py:30
  154.8 2.1 %collective-permute-done.7 = bf16[192,512]{1,0:T(8,128)(2,1)S(1)} collective-permute-done((bf16[192,512]{1,0:T(8,128)(2,1)S(1)}, bf16[192,512]{1,0:T(8,128)(2,1)S(1)}, u32[]{:S(2)}, u32[]{:S(2)}) %collective-permute-start.7) | collective-permute-done | bytes 196640 | tf_op jit(solution)/shard_map/ppermute | solution.py:30
  156.9 0.8 add_convert_fusion
Async XLA Ops:
  3.6 29.5 %copy-start.4 = (f32[96]{0:T(128)S(1)}, f32[96]{0:T(128)}, u32[]{:S(2)}) copy-start(f32[96]{0:T(128)} %param.12) | copy-start | bytes 1156
  3.6 29.6 %copy-start.5 = (f32[96]{0:T(128)S(1)}, f32[96]{0:T(128)}, u32[]{:S(2)}) copy-start(f32[96]{0:T(128)} %param.13) | copy-start | bytes 1156
  7.1 17.0 %collective-permute-start = (bf16[96,1,1,1024]{0,3,2,1:T(8,128)(2,1)S(1)}, bf16[96,1,1,1024]{0,3,2,1:T(8,128)(2,1)S(1)}, u32[]{:S(2)}, u32[]{:S(2)}) collective-permute-start(bf16[96,1,1,1024]{0,3,2,1:T(8,128)(2,1)S(1)} %select_bitcast_fusion), channel_id=1, source_target_pairs={{0,16},{16,32},{32,48},{48,64},{64,80},{80,96},{96,112},{112,128},... | collective-permute-start | bytes 589832 | tf_op jit(solution)/shard_map/ppermute | solution.py:21
  11.1 13.8 %collective-permute-start.1 = (bf16[96,1,1,1024]{0,3,2,1:T(8,128)(2,1)S(1)}, bf16[96,1,1,1024]{0,3,2,1:T(8,128)(2,1)S(1)}, u32[]{:S(2)}, u32[]{:S(2)}) collective-permute-start(bf16[96,1,1,1024]{0,3,2,1:T(8,128)(2,1)S(1)} %select_bitcast_fusion), channel_id=1, source_target_pairs={{16,0},{32,16},{48,32},{64,48},{80,64},{96,80},{112,96},{128,112},... | collective-permute-start | bytes 589832 | tf_op jit(solution)/shard_map/ppermute | solution.py:22
  25.3 12.7 %collective-permute-start.2 = (bf16[96,3,1,1024]{3,0,2,1:T(8,128)(2,1)S(1)}, bf16[96,3,1,1024]{3,0,2,1:T(8,128)(2,1)}, u32[]{:S(2)}, u32[]{:S(2)}) collective-permute-start(bf16[96,3,1,1024]{3,0,2,1:T(8,128)(2,1)S(1)} %copy.19), channel_id=1, source_target_pairs={{0,1},{1,2},{2,3},{3,4},{4,5},{5,6},{6,7},{7,8},{8,9},{9,10},{10,1... | collective-permute-start | bytes 1769480 | tf_op jit(solution)/shard_map/ppermute | solution.py:21
  31.2 12.4 %collective-permute-start.3 = (bf16[96,3,1,1024]{3,0,2,1:T(8,128)(2,1)S(1)}, bf16[96,3,1,1024]{3,0,2,1:T(8,128)(2,1)S(1)}, u32[]{:S(2)}, u32[]{:S(2)}) collective-permute-start(bf16[96,3,1,1024]{3,0,2,1:T(8,128)(2,1)S(1)} %copy.19), channel_id=1, source_target_pairs={{1,0},{2,1},{3,2},{4,3},{5,4},{6,5},{7,6},{8,7},{9,8},{10,9},{11,1... | collective-permute-start | bytes 1769480 | tf_op jit(solution)/shard_map/ppermute | solution.py:22
  45.8 2.9 %copy-start = (bf16[96,4096]{1,0:T(8,128)(2,1)S(1)}, bf16[96,4096]{1,0:T(8,128)(2,1)}, u32[]{:S(2)}) copy-start(bf16[96,4096]{1,0:T(8,128)(2,1)} %feat_ref.1) | copy-start | bytes 2359300
  45.8 2.9 %copy-start.1 = (bf16[27,96,96]{2,1,0:T(8,128)(2,1)S(1)}, bf16[27,96,96]{2,1,0:T(8,128)(2,1)}, u32[]{:S(2)}) copy-start(bf16[27,96,96]{2,1,0:T(8,128)(2,1)} %w_ref.1) | copy-start | bytes 1492996
  48.8 1.0 copy-start.2
  49.8 1.0 copy-start.3
  138.5 10.1 %collective-permute-start.6 = (bf16[192,512]{1,0:T(8,128)(2,1)S(1)}, bf16[192,512]{1,0:T(8,128)(2,1)S(1)}, u32[]{:S(2)}, u32[]{:S(2)}) collective-permute-start(bf16[192,512]{1,0:T(8,128)(2,1)S(1)} %get-tuple-element.7), channel_id=1, source_target_pairs={{16,0},{32,16},{48,32},{64,48},{80,64},{96,80},{112,96},{128,112},... | collective-permute-start | bytes 589832 | tf_op jit(solution)/shard_map/ppermute | solution.py:30
  144.7 6.4 %collective-permute-start.4 = (bf16[192,512]{1,0:T(8,128)(2,1)S(1)}, bf16[192,512]{1,0:T(8,128)(2,1)S(1)}, u32[]{:S(2)}, u32[]{:S(2)}) collective-permute-start(bf16[192,512]{1,0:T(8,128)(2,1)S(1)} %get-tuple-element.6), channel_id=1, source_target_pairs={{16,0},{32,16},{48,32},{64,48},{80,64},{96,80},{112,96},{128,112},... | collective-permute-start | bytes 589832 | tf_op jit(solution)/shard_map/ppermute | solution.py:30
  146.6 8.2 %collective-permute-start.5 = (bf16[192,512]{1,0:T(8,128)(2,1)S(1)}, bf16[192,512]{1,0:T(8,128)(2,1)S(1)}, u32[]{:S(2)}, u32[]{:S(2)}) collective-permute-start(bf16[192,512]{1,0:T(8,128)(2,1)S(1)} %get-tuple-element.8), channel_id=1, source_target_pairs={{1,0},{2,1},{3,2},{4,3},{5,4},{6,5},{7,6},{8,7},{9,8},{10,9},{11,1... | collective-permute-start | bytes 589832 | tf_op jit(solution)/shard_map/ppermute | solution.py:30
  148.6 8.4 %collective-permute-start.7 = (bf16[192,512]{1,0:T(8,128)(2,1)S(1)}, bf16[192,512]{1,0:T(8,128)(2,1)S(1)}, u32[]{:S(2)}, u32[]{:S(2)}) collective-permute-start(bf16[192,512]{1,0:T(8,128)(2,1)S(1)} %collective-permute-done.6), channel_id=1, source_target_pairs={{1,0},{2,1},{3,2},{4,3},{5,4},{6,5},{7,6},{8,7},{9,8},{10,9},{11,1... | collective-permute-start | bytes 589832 | tf_op jit(solution)/shard_map/ppermute | solution.py:30

commit v2 on v1

v2 whole, which is shorter than its diff:
```python
import jax
import jax.numpy as jnp
from jax import lax
from jax.experimental import pallas as pl
from jax.experimental.pallas import tpu as pltpu
from jax.sharding import PartitionSpec as P

F32 = jnp.float32
BF16 = jnp.bfloat16
LANES = 128
QC = 512
PARTS = 2
MESH = pl.DeviceIdType.MESH


def dot_nt(a, b):
    return lax.dot_general(a, b, (((1,), (1,)), ((), ())), preferred_element_type=F32)


def eye(rows, cols):
    r = lax.broadcasted_iota(jnp.int32, (rows, cols), 0)
    c = lax.broadcasted_iota(jnp.int32, (rows, cols), 1)
    return (r == c).astype(BF16)


def conv_kernel(
    nx, ny,
    send_ref, dest_ref, map_ref, feat_ref, w_ref, gain_ref, bias_ref, down_ref,
    fine_ref, coarse_ref,
    idx_a, idx_b, tiles, table, offered, halo, wpair, acc, part, out_x, in_x, out_y, in_y,
    idx_sem, halo_send, halo_recv, x_send, x_recv, y_send, y_recv,
    ga0, ga1, gb0, gb1,
):
    channels, slots = feat_ref.shape
    bnd = halo.shape[2]
    koff = map_ref.shape[0]
    centre = koff // 2
    others = [k for k in range(koff) if k != centre]
    pairs = len(others) // 2
    blocks = slots // QC
    total = blocks * pairs
    lane_tiles = QC // LANES
    coarse_len = slots // 8
    halves = 8 // lane_tiles
    chunks = blocks // halves
    out_channels = part.shape[1]
    idx = (idx_a, idx_b)
    rows = ((ga0, ga1), (gb0, gb1))

    i, j = lax.axis_index("gx"), lax.axis_index("gy")
    has_left, has_right = i > 0, i < nx - 1
    has_down, has_up = j > 0, j < ny - 1
    around = (
        (has_left, (i - 1, j)),
        (has_right, (i + 1, j)),
        (has_down, (i, j - 1)),
        (has_up, (i, j + 1)),
    )

    halo[...] = jnp.zeros_like(halo)
    in_x[...] = jnp.zeros_like(in_x)
    in_y[...] = jnp.zeros_like(in_y)

    barrier = pltpu.get_barrier_semaphore()
    for there, device in around:
        @pl.when(there)
        def _():
            pl.semaphore_signal(barrier, inc=1, device_id=device, device_id_type=MESH)

    step = 256
    ident = eye(step, step)
    pad = jnp.zeros((LANES - channels, step), BF16)

    def own_rows(n, _):
        c0 = pl.multiple_of(n * step, step)
        x = jnp.concatenate([feat_ref[:, pl.ds(c0, step)], pad], axis=0)
        table[pl.ds(c0, step), :] = dot_nt(ident, x)
        return 0

    lax.fori_loop(0, slots // step, own_rows, 0, unroll=2)
    table[pl.ds(slots + 9 * bnd, 8), :] = jnp.zeros((8, LANES), F32)

    for r in range(bnd):
        offered[pl.ds(r, 1), :] = table[pl.ds(send_ref[r], 1), :]
    halo[4] = dot_nt(eye(channels, LANES), offered[...].astype(BF16)).astype(BF16)

    pl.semaphore_wait(barrier, sum(there.astype(jnp.int32) for there, _ in around))

    right, left, up, down = (i + 1, j), (i - 1, j), (i, j + 1), (i, j - 1)
    both = jnp.logical_and
    sends = (
        (4, 1, right, has_right, has_left),
        (4, 7, left, has_left, has_right),
        (4, 3, up, has_up, has_down),
        (4, 5, down, has_down, has_up),
        (1, 0, up, both(has_left, has_up), both(has_left, has_down)),
        (1, 2, down, both(has_left, has_down), both(has_left, has_up)),
        (7, 6, up, both(has_right, has_up), both(has_right, has_down)),
        (7, 8, down, both(has_right, has_down), both(has_right, has_up)),
    )
    depth = channels // PARTS

    def boundary(n, piece):
        src, dst, device, _, _ = sends[n]
        span = pl.ds(piece * depth, depth)
        return pltpu.make_async_remote_copy(
            src_ref=halo.at[src, span],
            dst_ref=halo.at[dst, span],
            send_sem=halo_send.at[n, piece],
            recv_sem=halo_recv.at[n, piece],
            device_id=device,
            device_id_type=MESH,
        )

    def start(n, piece):
        @pl.when(sends[n][3])
        def _():
            boundary(n, piece).start()

    def arrived(n, piece):
        @pl.when(sends[n][4])
        def _():
            boundary(n, piece).wait_recv()

    for piece in range(PARTS):
        for n in range(4):
            start(n, piece)

    wpair[...] = jnp.zeros_like(wpair)
    for n, k in enumerate(others):
        wpair[n // 2, :, pl.ds((n % 2) * LANES, channels)] = w_ref[k]

    def first_col(b, t):
        return ((b % halves) * lane_tiles + t) * coarse_len + (b // halves) * LANES

    for b in range(blocks):
        for m in range(pairs):
            for h in range(2):
                for t in range(lane_tiles):
                    tiles[b * pairs + m, pl.ds(h * lane_tiles + t, 1), :] = map_ref[
                        pl.ds(others[2 * m + h], 1), pl.ds(first_col(b, t), LANES)
                    ]

    def tile_rows(t):
        for n in range(bnd // step):
            x = jnp.concatenate([halo[t, :, pl.ds(n * step, step)], pad], axis=0)
            table[pl.ds(slots + t * bnd + n * step, step), :] = dot_nt(ident, x)

    tile_rows(4)
    for piece in range(PARTS):
        arrived(0, piece)
        start(4, piece)
        start(5, piece)
        arrived(1, piece)
        start(6, piece)
        start(7, piece)
    tile_rows(1)
    tile_rows(7)
    for n in range(2, 8):
        for piece in range(PARTS):
            arrived(n, piece)
        tile_rows(sends[n][1])

    def fetch(t, s):
        return pltpu.make_async_copy(tiles.at[t], idx[s], idx_sem.at[s])

    def gather(s):
        for h in range(2):
            for r in range(QC):
                at = idx[s][h * lane_tiles + r // LANES, r % LANES]
                rows[s][h][pl.ds(r, 1), :] = table[pl.ds(at, 1), :]

    def multiply(t, s):
        m = lax.rem(t, pairs)
        g = jnp.concatenate([rows[s][0][...], rows[s][1][...]], axis=1).astype(BF16)
        keep = jnp.where(m == 0, 0.0, 1.0)
        acc[...] = acc[...] * keep + dot_nt(wpair[m], g)

    dest = dest_ref[0]
    out_x[:, pl.ds(out_channels, 16), :] = jnp.full(
        (chunks, 16, LANES), dest.astype(F32), F32
    ).astype(BF16)

    def to_left(v):
        return pltpu.make_async_remote_copy(
            src_ref=out_x.at[v], dst_ref=in_x.at[v],
            send_sem=x_send.at[v], recv_sem=x_recv.at[v],
            device_id=left, device_id_type=MESH,
        )

    def to_down(v):
        return pltpu.make_async_remote_copy(
            src_ref=out_y.at[v], dst_ref=in_y.at[v],
            send_sem=y_send.at[v], recv_sem=y_recv.at[v],
            device_id=down, device_id_type=MESH,
        )

    def from_right(v, which):
        got = in_x[v].astype(F32)
        kind = got[out_channels : out_channels + 1]
        return jnp.where(kind == float(which), got[:out_channels], 0.0)

    def finish(t):
        b = lax.div(t, pairs)

        @pl.when(t - b * pairs == pairs - 1)
        def _():
            v = lax.div(b, halves)
            half = b - v * halves
            new = jnp.zeros((out_channels, LANES), F32)
            for u in range(lane_tiles):
                p = half * lane_tiles + u
                cols = pl.ds(pl.multiple_of(p * coarse_len + v * LANES, LANES), LANES)
                conv = acc[:, u * LANES : (u + 1) * LANES] + jnp.dot(
                    w_ref[centre], feat_ref[:, cols], preferred_element_type=F32
                )
                active = (map_ref[centre : centre + 1, cols] < slots).astype(F32)
                fine = jnp.maximum(conv * gain_ref[...] + bias_ref[...], 0.0) * active
                fine = fine.astype(BF16)
                fine_ref[:, cols] = fine
                new = new + jnp.dot(down_ref[p], fine, preferred_element_type=F32)
            part[v] = part[v] + new

            @pl.when(half == halves - 1)
            def _():
                out_x[v, pl.ds(0, out_channels), :] = part[v].astype(BF16)

                @pl.when(has_left)
                def _():
                    to_left(v).start()

    def onwards(v):
        @pl.when(has_right)
        def _():
            to_left(v).wait_recv()

        out_y[v] = (jnp.where(dest == 2, part[v], 0.0) + from_right(v, 3)).astype(BF16)

        @pl.when(has_down)
        def _():
            to_down(v).start()

    part[...] = jnp.zeros_like(part)
    acc[...] = jnp.zeros_like(acc)
    fetch(0, 0).start()
    fetch(1, 1).start()
    fetch(0, 0).wait()
    gather(0)
    fetch(2, 0).start()

    def body(n, _):
        for s in (1, 0):
            t = 2 * n + (1 if s == 1 else 2)
            fetch(t, s).wait()
            multiply(t - 1, 1 - s)
            gather(s)
            fetch(jnp.minimum(t + 2, total - 1), s).start()
            finish(t - 1)
        per_chunk = pairs * halves
        v = lax.div(2 * n, per_chunk)

        @pl.when(jnp.logical_and(v > 0, 2 * n - v * per_chunk == pairs - 1))
        def _():
            onwards(v - 1)

        return 0

    lax.fori_loop(0, (total - 2) // 2, body, 0)
    fetch(total - 1, 1).wait()
    multiply(total - 2, 0)
    gather(1)
    finish(total - 2)
    multiply(total - 1, 1)
    finish(total - 1)
    fetch(total - 1, 0).wait()

    onwards(chunks - 1)
    for v in range(chunks):
        @pl.when(has_up)
        def _():
            to_down(v).wait_recv()

        coarse_ref[:, pl.ds(v * LANES, LANES)] = (
            jnp.where(dest == 0, part[v], 0.0) + from_right(v, 1) + in_y[v].astype(F32)
        ).astype(BF16)

    for n in range(8):
        @pl.when(sends[n][3])
        def _():
            for piece in range(PARTS):
                boundary(n, piece).wait_send()
    for v in range(chunks):
        @pl.when(has_left)
        def _():
            to_left(v).wait_send()

        @pl.when(has_down)
        def _():
            to_down(v).wait_send()


def shards(
    features, kernel_map, send_rows, conv_weight, conv_gain, conv_bias, down_weight, coarse_dest
):
    channels, slots = features.shape
    bnd = send_rows.shape[0]
    koff = kernel_map.shape[0]
    pairs = koff // 2
    total = slots // QC * pairs
    out_channels = down_weight.shape[1]
    coarse_len = slots // 8
    chunks = coarse_len // LANES
    nx, ny = lax.axis_size("gx"), lax.axis_size("gy")
    vmem = pl.BlockSpec(memory_space=pltpu.VMEM)
    smem = pl.BlockSpec(memory_space=pltpu.SMEM)

    def kernel(*refs):
        conv_kernel(nx, ny, *refs)

    fine, coarse = pl.pallas_call(
        kernel,
        in_specs=[smem] * 2 + [vmem] * 6,
        out_specs=[vmem] * 2,
        out_shape=[
            jax.ShapeDtypeStruct((channels, slots), BF16),
            jax.ShapeDtypeStruct((out_channels, coarse_len), BF16),
        ],
        scratch_shapes=[
            pltpu.SMEM((8, LANES), jnp.int32),
            pltpu.SMEM((8, LANES), jnp.int32),
            pltpu.VMEM((total, 8, LANES), jnp.int32),
            pltpu.VMEM((slots + 9 * bnd + 8, LANES), F32),
            pltpu.VMEM((bnd, LANES), F32),
            pltpu.VMEM((9, channels, bnd), BF16),
            pltpu.VMEM((pairs, channels, 2 * LANES), BF16),
            pltpu.VMEM((channels, QC), F32),
            pltpu.VMEM((chunks, out_channels, LANES), F32),
            pltpu.VMEM((chunks, out_channels + 16, LANES), BF16),
            pltpu.VMEM((chunks, out_channels + 16, LANES), BF16),
            pltpu.VMEM((chunks, out_channels, LANES), BF16),
            pltpu.VMEM((chunks, out_channels, LANES), BF16),
            pltpu.SemaphoreType.DMA((2,)),
            pltpu.SemaphoreType.DMA((8, PARTS)),
            pltpu.SemaphoreType.DMA((8, PARTS)),
            pltpu.SemaphoreType.DMA((chunks,)),
            pltpu.SemaphoreType.DMA((chunks,)),
            pltpu.SemaphoreType.DMA((chunks,)),
            pltpu.SemaphoreType.DMA((chunks,)),
        ]
        + [pltpu.VMEM((QC, LANES), F32)] * 4,
        compiler_params=pltpu.CompilerParams(
            vmem_limit_bytes=48 * 2**20, collective_id=0, has_side_effects=True
        ),
        name="sparse_conv",
    )(
        send_rows, coarse_dest, kernel_map, features, conv_weight,
        conv_gain[:, None], conv_bias[:, None], down_weight,
    )
    return (fine, coarse)


def solution(mesh):
    placed = (
        P(None, ("gx", "gy")),
        P(None, ("gx", "gy")),
        P(("gx", "gy")),
        P(),
        P(),
        P(),
        P(),
        P(("gx", "gy")),
    )
    return jax.shard_map(
        shards,
        mesh=mesh,
        in_specs=placed,
        out_specs=(P(None, ("gx", "gy")), P(None, ("gx", "gy"))),
        check_vma=False,
    )
```

time: 158 us -> 115 us (0.73)
  starting transfers between devices: 32.6 us -> 0 us
  waiting for transfers between devices: 19.5 us -> 0 us
  Pallas kernels: 87.5 us -> 106 us
  other arithmetic: 4.49 us -> 0 us
  local copies, waits for them, and re-layouts: 12.1 us -> 7.81 us
    ppermute x8 -> x0, starting transfers between devices: 32.6 us -> none  [the longest x4 12 us: passed_along(): return lax.ppermute(shard, axis, pairs)]
    ppermute x8 -> x0, waiting for transfers between devices: 19.5 us -> none  [the longest x2 8.08 us: padded(): before = lax.ppermute(last, axis, up)]
    pallas_call x1, Pallas kernels: 87.5 us -> 106 us  [shards(): pl.pallas_call(kernel, in_specs=[smem] * 2 + [vmem] * 6, out_specs=[vmem]...]
    unnamed x13 -> x16, local copies, waits for them, and re-layouts: 3.62 us -> 7.6 us
    gather x1 -> x0, local copies, waits for them, and re-layouts: 3.21 us -> none  [shards(): boundary = jnp.take(feature_rows, send_rows, axis=0)]
    reshape x1 -> x0, local copies, waits for them, and re-layouts: 2.93 us -> none  [shards(): padded(boundary, (('gx', 1), ('gy', 2)), 1)]
    concatenate x2 -> x0, other arithmetic: 2.02 us -> none  [padded(): shard = jnp.concatenate([before, shard, after], axis=dim)]
    ppermute x2 -> x0, local copies, waits for them, and re-layouts: 1.81 us -> none  [the longest x1 1.44 us: padded(): before = lax.ppermute(last, axis, up)]
  transfers between devices with their start and end apart: 8 -> 0, of which waited for: 7 -> 0; matrix products, arithmetic and copies ran while one was open for 1% -> 0% of each run, Pallas kernels for 0% -> 0%
where the time goes in v2:
time: 115 us
  Pallas kernels  106 us (92%)
  local copies, waits for them, and re-layouts  7.81 us (7%)
  between operations  1.3 us (1%)
    pallas_call x1, Pallas kernels, shards(): pl.pallas_call(kernel, in_specs=[smem] * 2 + [vmem] * 6, out_specs=[vmem]...  106 us
    unnamed x16, local copies, waits for them, and re-layouts  7.6 us

profile of v2, /device:TPU:31, one launch (start us, length us, event | category | flops | bytes accessed | tf_op | source)
XLA Modules:
  0.0 115.0 jit_solution(6530006847848156633)
XLA Ops:
  1.3 0.0 copy-start.5
  1.3 0.6 copy-done.5
  1.9 0.0 copy-start.6
  1.9 0.1 copy.10.refs_5_
  2.0 0.5 copy-done.6
  2.6 0.0 copy-start.4
  2.6 0.1 copy.11.refs_6_
  2.7 0.6 copy-done.4
  3.3 0.0 copy-start
  3.3 1.1 copy-done
  4.4 0.0 copy-start.1
  4.4 1.1 copy-done.1
  5.5 0.0 copy-start.2
  5.5 1.0 copy-done.2
  6.5 0.0 copy-start.3
  6.5 1.0 copy-done.3
  7.5 105.9 %sparse_conv.1 = (bf16[96,4096]{1,0:T(8,128)(2,1)S(1)}, bf16[192,512]{1,0:T(8,128)(2,1)S(1)}) custom-call(s32[1024]{0:T(1024)S(1)} %copy-done.4, s32[1]{0:T(128)S(6)} %copy.14.refs_1_, s32[27,4096]{1,0:T(8,128)S(1)} %copy-done.2, bf16[96,4096]{1,0:T(8,128)(2,1)S(1)} %copy-done, bf16[27,96,96]{2,1,0:T(8,128)(2,1)S(1)} %copy-done.1, ...), custom_call_target="tpu_custom_call" | custom-call | tf_op jit(solution)/shard_map/sparse_conv/pallas_call | solution.py:320
  113.5 0.9 copy.15
  114.4 0.7 copy.16
Async XLA Ops:
  1.3 0.7 copy-start.5
  1.9 0.7 copy-start.6
  2.6 0.7 copy-start.4
  3.3 1.1 copy-start
  4.4 1.1 copy-start.1
  5.5 1.0 copy-start.2
  6.5 1.0 copy-start.3

commit v3 on v2

--- a/solution.py
+++ b/solution.py
@@ -8,8 +8,8 @@
 F32 = jnp.float32
 BF16 = jnp.bfloat16
 LANES = 128
-QC = 512
-PARTS = 2
+QC = 1024
+PARTS = 3
 MESH = pl.DeviceIdType.MESH
 
 
@@ -25,12 +25,28 @@
 
 def conv_kernel(
     nx, ny,
-    send_ref, dest_ref, map_ref, feat_ref, w_ref, gain_ref, bias_ref, down_ref,
-    fine_ref, coarse_ref,
+    dest_ref, *refs,
+):
+    hbm, refs = refs[:7], refs[7:]
+    fine_ref, coarse_ref = refs[:2]
+    here, in_sem = refs[2:9], refs[9]
+    compute(nx, ny, dest_ref, fine_ref, coarse_ref, hbm, here, in_sem, *refs[10:])
+
+
+def compute(
+    nx, ny, dest_ref, fine_ref, coarse_ref, hbm, here, in_sem,
     idx_a, idx_b, tiles, table, offered, halo, wpair, acc, part, out_x, in_x, out_y, in_y,
     idx_sem, halo_send, halo_recv, x_send, x_recv, y_send, y_recv,
-    ga0, ga1, gb0, gb1,
+    gain_ref, bias_ref,
 ):
+    send_ref, map_ref, feat_ref, w_ref, gain_row, bias_row, down_ref = here
+    send_n, map_n, feat_n, w_n, gain_n, bias_n, down_n = range(7)
+
+    def load(n):
+        return pltpu.make_async_copy(hbm[n], here[n], in_sem.at[n])
+
+    for n in (feat_n, send_n, w_n, map_n, gain_n, bias_n, down_n):
+        load(n).start()
     channels, slots = feat_ref.shape
     bnd = halo.shape[2]
     koff = map_ref.shape[0]
@@ -45,7 +61,6 @@
     chunks = blocks // halves
     out_channels = part.shape[1]
     idx = (idx_a, idx_b)
-    rows = ((ga0, ga1), (gb0, gb1))
 
     i, j = lax.axis_index("gx"), lax.axis_index("gy")
     has_left, has_right = i > 0, i < nx - 1
@@ -57,9 +72,14 @@
         (has_up, (i, j + 1)),
     )
 
-    halo[...] = jnp.zeros_like(halo)
-    in_x[...] = jnp.zeros_like(in_x)
-    in_y[...] = jnp.zeros_like(in_y)
+    both = jnp.logical_and
+    inner = both(both(has_left, has_right), both(has_down, has_up))
+
+    @pl.when(jnp.logical_not(inner))
+    def _():
+        halo[...] = jnp.zeros_like(halo)
+        in_x[...] = jnp.zeros_like(in_x)
+        in_y[...] = jnp.zeros_like(in_y)
 
     barrier = pltpu.get_barrier_semaphore()
     for there, device in around:
@@ -77,9 +97,11 @@
         table[pl.ds(c0, step), :] = dot_nt(ident, x)
         return 0
 
-    lax.fori_loop(0, slots // step, own_rows, 0, unroll=2)
+    load(feat_n).wait()
+    lax.fori_loop(0, slots // step, own_rows, 0, unroll=8)
     table[pl.ds(slots + 9 * bnd, 8), :] = jnp.zeros((8, LANES), F32)
 
+    load(send_n).wait()
     for r in range(bnd):
         offered[pl.ds(r, 1), :] = table[pl.ds(send_ref[r], 1), :]
     halo[4] = dot_nt(eye(channels, LANES), offered[...].astype(BF16)).astype(BF16)
@@ -87,7 +109,6 @@
     pl.semaphore_wait(barrier, sum(there.astype(jnp.int32) for there, _ in around))
 
     right, left, up, down = (i + 1, j), (i - 1, j), (i, j + 1), (i, j - 1)
-    both = jnp.logical_and
     sends = (
         (4, 1, right, has_right, has_left),
         (4, 7, left, has_left, has_right),
@@ -126,9 +147,18 @@
         for n in range(4):
             start(n, piece)
 
+    load(w_n).wait()
     wpair[...] = jnp.zeros_like(wpair)
     for n, k in enumerate(others):
         wpair[n // 2, :, pl.ds((n % 2) * LANES, channels)] = w_ref[k]
+
+    load(gain_n).wait()
+    load(bias_n).wait()
+    for row, column in ((gain_row, gain_ref), (bias_row, bias_ref)):
+        spread = jnp.where(eye(channels, channels) > 0, row[...], 0.0)
+        column[...] = jnp.sum(spread, axis=1, keepdims=True)
+    load(down_n).wait()
+    load(map_n).wait()
 
     def first_col(b, t):
         return ((b % halves) * lane_tiles + t) * coarse_len + (b // halves) * LANES
@@ -164,17 +194,21 @@
     def fetch(t, s):
         return pltpu.make_async_copy(tiles.at[t], idx[s], idx_sem.at[s])
 
-    def gather(s):
-        for h in range(2):
-            for r in range(QC):
-                at = idx[s][h * lane_tiles + r // LANES, r % LANES]
-                rows[s][h][pl.ds(r, 1), :] = table[pl.ds(at, 1), :]
-
-    def multiply(t, s):
+    def gather_multiply(t, s):
         m = lax.rem(t, pairs)
-        g = jnp.concatenate([rows[s][0][...], rows[s][1][...]], axis=1).astype(BF16)
         keep = jnp.where(m == 0, 0.0, 1.0)
-        acc[...] = acc[...] * keep + dot_nt(wpair[m], g)
+        for u in range(lane_tiles):
+            sides = []
+            for h in range(2):
+                at = [idx[s][h * lane_tiles + u, r] for r in range(LANES)]
+                eights = [
+                    jnp.concatenate([table[pl.ds(a, 1), :] for a in at[r : r + 8]], axis=0)
+                    for r in range(0, LANES, 8)
+                ]
+                sides.append(jnp.concatenate(eights, axis=0))
+            g = jnp.concatenate(sides, axis=1).astype(BF16)
+            cols = slice(u * LANES, (u + 1) * LANES)
+            acc[:, cols] = acc[:, cols] * keep + dot_nt(wpair[m], g)
 
     dest = dest_ref[0]
     out_x[:, pl.ds(out_channels, 16), :] = jnp.full(
@@ -219,7 +253,7 @@
                 fine = fine.astype(BF16)
                 fine_ref[:, cols] = fine
                 new = new + jnp.dot(down_ref[p], fine, preferred_element_type=F32)
-            part[v] = part[v] + new
+            part[v] = part[v] * jnp.where(half == 0, 0.0, 1.0) + new
 
             @pl.when(half == halves - 1)
             def _():
@@ -244,35 +278,25 @@
     acc[...] = jnp.zeros_like(acc)
     fetch(0, 0).start()
     fetch(1, 1).start()
-    fetch(0, 0).wait()
-    gather(0)
-    fetch(2, 0).start()
 
     def body(n, _):
-        for s in (1, 0):
-            t = 2 * n + (1 if s == 1 else 2)
+        for s in range(2):
+            t = 2 * n + s
             fetch(t, s).wait()
-            multiply(t - 1, 1 - s)
-            gather(s)
+            gather_multiply(t, s)
             fetch(jnp.minimum(t + 2, total - 1), s).start()
-            finish(t - 1)
-        per_chunk = pairs * halves
-        v = lax.div(2 * n, per_chunk)
-
-        @pl.when(jnp.logical_and(v > 0, 2 * n - v * per_chunk == pairs - 1))
+            finish(t)
+        v = lax.div(2 * n, pairs * halves)
+
+        @pl.when(both(v > 0, lax.div(2 * n - v * pairs * halves, 2) == pairs // 4))
         def _():
             onwards(v - 1)
 
         return 0
 
-    lax.fori_loop(0, (total - 2) // 2, body, 0)
+    lax.fori_loop(0, total // 2, body, 0)
+    fetch(total - 1, 0).wait()
     fetch(total - 1, 1).wait()
-    multiply(total - 2, 0)
-    gather(1)
-    finish(total - 2)
-    multiply(total - 1, 1)
-    finish(total - 1)
-    fetch(total - 1, 0).wait()
 
     onwards(chunks - 1)
     for v in range(chunks):
@@ -319,16 +343,24 @@
 
     fine, coarse = pl.pallas_call(
         kernel,
-        in_specs=[smem] * 2 + [vmem] * 6,
+        in_specs=[smem] + [pl.BlockSpec(memory_space=pltpu.HBM)] * 7,
         out_specs=[vmem] * 2,
         out_shape=[
             jax.ShapeDtypeStruct((channels, slots), BF16),
             jax.ShapeDtypeStruct((out_channels, coarse_len), BF16),
         ],
         scratch_shapes=[
-            pltpu.SMEM((8, LANES), jnp.int32),
-            pltpu.SMEM((8, LANES), jnp.int32),
-            pltpu.VMEM((total, 8, LANES), jnp.int32),
+            pltpu.SMEM((bnd,), jnp.int32),
+            pltpu.VMEM(kernel_map.shape, jnp.int32),
+            pltpu.VMEM(features.shape, BF16),
+            pltpu.VMEM(conv_weight.shape, BF16),
+            pltpu.VMEM((1, channels), F32),
+            pltpu.VMEM((1, channels), F32),
+            pltpu.VMEM(down_weight.shape, BF16),
+            pltpu.SemaphoreType.DMA((7,)),
+            pltpu.SMEM((2 * QC // LANES, LANES), jnp.int32),
+            pltpu.SMEM((2 * QC // LANES, LANES), jnp.int32),
+            pltpu.VMEM((total, 2 * QC // LANES, LANES), jnp.int32),
             pltpu.VMEM((slots + 9 * bnd + 8, LANES), F32),
             pltpu.VMEM((bnd, LANES), F32),
             pltpu.VMEM((9, channels, bnd), BF16),
@@ -347,14 +379,14 @@
             pltpu.SemaphoreType.DMA((chunks,)),
             pltpu.SemaphoreType.DMA((chunks,)),
         ]
-        + [pltpu.VMEM((QC, LANES), F32)] * 4,
+        + [pltpu.VMEM((channels, 1), F32)] * 2,
         compiler_params=pltpu.CompilerParams(
-            vmem_limit_bytes=48 * 2**20, collective_id=0, has_side_effects=True
+            vmem_limit_bytes=61 * 2**20, collective_id=0, has_side_effects=True
         ),
         name="sparse_conv",
     )(
-        send_rows, coarse_dest, kernel_map, features, conv_weight,
-        conv_gain[:, None], conv_bias[:, None], down_weight,
+        coarse_dest, send_rows, kernel_map, features, conv_weight,
+        conv_gain[None, :], conv_bias[None, :], down_weight,
     )
     return (fine, coarse)
 

time: 115 us -> 101 us (0.88)
  Pallas kernels: 106 us -> 97 us
  local copies, waits for them, and re-layouts: 7.81 us -> 2.78 us
    pallas_call x1, Pallas kernels: 106 us -> 97 us  [shards(): pl.pallas_call(kernel, in_specs=[smem] + [pl.BlockSpec(memory_space=pltpu...]
    unnamed x16 -> x4, local copies, waits for them, and re-layouts: 7.6 us -> 2.78 us
where the time goes in v3:
time: 101 us
  Pallas kernels  97 us (96%)
  local copies, waits for them, and re-layouts  2.78 us (3%)
  between operations  1.3 us (1%)
    pallas_call x1, Pallas kernels, shards(): pl.pallas_call(kernel, in_specs=[smem] + [pl.BlockSpec(memory_space=pltpu...  97 us
    unnamed x4, local copies, waits for them, and re-layouts  2.78 us

profile of v3, /device:TPU:31, one launch (start us, length us, event | category | flops | bytes accessed | tf_op | source)
XLA Modules:
  0.0 101.0 jit_solution(17638304104715323431)
XLA Ops:
  1.3 97.0 %sparse_conv.1 = (bf16[96,4096]{1,0:T(8,128)(2,1)}, bf16[192,512]{1,0:T(8,128)(2,1)}) custom-call(s32[1]{0:T(128)S(6)} %copy.12.refs_0_, s32[1024]{0:T(1024)} %refs_1_.1, s32[27,4096]{1,0:T(8,128)} %refs_2_.1, bf16[96,4096]{1,0:T(8,128)(2,1)} %refs_3_.1, bf16[27,96,96]{2,1,0:T(8,128)(2,1)} %refs_4_.1, f32[1,96]{1,0:T(1,128)} %bitcast.2, f32[1,96]{1,0:T(1,128)} %bitcast.3, ...), custom_call_target="tpu_custom_call" | custom-call | tf_op jit(solution)/shard_map/sparse_conv/pallas_call | solution.py:344
  98.2 0.0 copy-start
  98.3 2.1 %copy.13 = bf16[96,4096]{1,0:T(8,128)(2,1)} copy(bf16[96,4096]{1,0:T(8,128)(2,1)} %get-tuple-element.4) | data formatting | bytes 1572864
  100.4 0.0 copy-done
  100.4 0.7 copy.14
Async XLA Ops:
  98.2 2.1 %copy-start = (bf16[192,512]{1,0:T(8,128)(2,1)S(1)}, bf16[192,512]{1,0:T(8,128)(2,1)}, u32[]{:S(2)}) copy-start(bf16[192,512]{1,0:T(8,128)(2,1)} %get-tuple-element.5) | copy-start | bytes 589828

commit v4 on v3

--- a/solution.py
+++ b/solution.py
@@ -9,6 +9,7 @@
 BF16 = jnp.bfloat16
 LANES = 128
 QC = 1024
+STEP = 2
 PARTS = 3
 MESH = pl.DeviceIdType.MESH
 
@@ -167,7 +168,11 @@
         for m in range(pairs):
             for h in range(2):
                 for t in range(lane_tiles):
-                    tiles[b * pairs + m, pl.ds(h * lane_tiles + t, 1), :] = map_ref[
+                    tiles[
+                        (b * pairs + m) // STEP,
+                        pl.ds((b * pairs + m) % STEP * 2 * lane_tiles + h * lane_tiles + t, 1),
+                        :,
+                    ] = map_ref[
                         pl.ds(others[2 * m + h], 1), pl.ds(first_col(b, t), LANES)
                     ]
 
@@ -194,13 +199,15 @@
     def fetch(t, s):
         return pltpu.make_async_copy(tiles.at[t], idx[s], idx_sem.at[s])
 
-    def gather_multiply(t, s):
-        m = lax.rem(t, pairs)
+    def gather_multiply(t, s, e):
+        b = lax.div(t, pairs)
+        m = t - b * pairs
         keep = jnp.where(m == 0, 0.0, 1.0)
+        first = e * 2 * lane_tiles
         for u in range(lane_tiles):
             sides = []
             for h in range(2):
-                at = [idx[s][h * lane_tiles + u, r] for r in range(LANES)]
+                at = [idx[s][first + h * lane_tiles + u, r] for r in range(LANES)]
                 eights = [
                     jnp.concatenate([table[pl.ds(a, 1), :] for a in at[r : r + 8]], axis=0)
                     for r in range(0, LANES, 8)
@@ -208,7 +215,7 @@
                 sides.append(jnp.concatenate(eights, axis=0))
             g = jnp.concatenate(sides, axis=1).astype(BF16)
             cols = slice(u * LANES, (u + 1) * LANES)
-            acc[:, cols] = acc[:, cols] * keep + dot_nt(wpair[m], g)
+            acc[b, :, cols] = acc[b, :, cols] * keep + dot_nt(wpair[m], g)
 
     dest = dest_ref[0]
     out_x[:, pl.ds(out_channels, 16), :] = jnp.full(
@@ -245,7 +252,7 @@
             for u in range(lane_tiles):
                 p = half * lane_tiles + u
                 cols = pl.ds(pl.multiple_of(p * coarse_len + v * LANES, LANES), LANES)
-                conv = acc[:, u * LANES : (u + 1) * LANES] + jnp.dot(
+                conv = acc[b, :, u * LANES : (u + 1) * LANES] + jnp.dot(
                     w_ref[centre], feat_ref[:, cols], preferred_element_type=F32
                 )
                 active = (map_ref[centre : centre + 1, cols] < slots).astype(F32)
@@ -279,24 +286,30 @@
     fetch(0, 0).start()
     fetch(1, 1).start()
 
+    steps = total // STEP
+
     def body(n, _):
         for s in range(2):
-            t = 2 * n + s
-            fetch(t, s).wait()
-            gather_multiply(t, s)
-            fetch(jnp.minimum(t + 2, total - 1), s).start()
-            finish(t)
-        v = lax.div(2 * n, pairs * halves)
-
-        @pl.when(both(v > 0, lax.div(2 * n - v * pairs * halves, 2) == pairs // 4))
+            step_now = 2 * n + s
+            fetch(step_now, s).wait()
+            for e in range(STEP):
+                gather_multiply(step_now * STEP + e, s, e)
+            fetch(jnp.minimum(step_now + 2, steps - 1), s).start()
+            for e in range(STEP):
+                finish(step_now * STEP + e)
+        t = 2 * STEP * n
+        v = lax.div(t, pairs * halves)
+        since = t - v * pairs * halves
+
+        @pl.when(both(v > 0, both(since >= 6, since < 6 + 2 * STEP)))
         def _():
             onwards(v - 1)
 
         return 0
 
-    lax.fori_loop(0, total // 2, body, 0)
-    fetch(total - 1, 0).wait()
-    fetch(total - 1, 1).wait()
+    lax.fori_loop(0, steps // 2, body, 0)
+    fetch(steps - 1, 0).wait()
+    fetch(steps - 1, 1).wait()
 
     onwards(chunks - 1)
     for v in range(chunks):
@@ -358,14 +371,14 @@
             pltpu.VMEM((1, channels), F32),
             pltpu.VMEM(down_weight.shape, BF16),
             pltpu.SemaphoreType.DMA((7,)),
-            pltpu.SMEM((2 * QC // LANES, LANES), jnp.int32),
-            pltpu.SMEM((2 * QC // LANES, LANES), jnp.int32),
-            pltpu.VMEM((total, 2 * QC // LANES, LANES), jnp.int32),
+            pltpu.SMEM((STEP * 2 * QC // LANES, LANES), jnp.int32),
+            pltpu.SMEM((STEP * 2 * QC // LANES, LANES), jnp.int32),
+            pltpu.VMEM((total // STEP, STEP * 2 * QC // LANES, LANES), jnp.int32),
             pltpu.VMEM((slots + 9 * bnd + 8, LANES), F32),
             pltpu.VMEM((bnd, LANES), F32),
             pltpu.VMEM((9, channels, bnd), BF16),
             pltpu.VMEM((pairs, channels, 2 * LANES), BF16),
-            pltpu.VMEM((channels, QC), F32),
+            pltpu.VMEM((slots // QC, channels, QC), F32),
             pltpu.VMEM((chunks, out_channels, LANES), F32),
             pltpu.VMEM((chunks, out_channels + 16, LANES), BF16),
             pltpu.VMEM((chunks, out_channels + 16, LANES), BF16),

time: 101 us -> 97.5 us (0.965)
  Pallas kernels: 97 us -> 93.3 us
    pallas_call x1, Pallas kernels: 97 us -> 93.3 us  [shards(): pl.pallas_call(kernel, in_specs=[smem] + [pl.BlockSpec(memory_space=pltpu...]
where the time goes in v4:
time: 97.5 us; the launch traced here: 97.3 us
  Pallas kernels  93.3 us (96%)
  local copies, waits for them, and re-layouts  2.78 us (3%)
  between operations  1.3 us (1%)
    pallas_call x1, Pallas kernels, shards(): pl.pallas_call(kernel, in_specs=[smem] + [pl.BlockSpec(memory_space=pltpu...  93.3 us
    unnamed x4, local copies, waits for them, and re-layouts  2.78 us

profile of v4, /device:TPU:31, one launch (start us, length us, event | category | flops | bytes accessed | tf_op | source)
XLA Modules:
  0.0 97.3 jit_solution(17966205536514342449)
XLA Ops:
  1.3 93.3 %sparse_conv.1 = (bf16[96,4096]{1,0:T(8,128)(2,1)}, bf16[192,512]{1,0:T(8,128)(2,1)}) custom-call(s32[1]{0:T(128)S(6)} %copy.12.refs_0_, s32[1024]{0:T(1024)} %refs_1_.1, s32[27,4096]{1,0:T(8,128)} %refs_2_.1, bf16[96,4096]{1,0:T(8,128)(2,1)} %refs_3_.1, bf16[27,96,96]{2,1,0:T(8,128)(2,1)} %refs_4_.1, f32[1,96]{1,0:T(1,128)} %bitcast.2, f32[1,96]{1,0:T(1,128)} %bitcast.3, ...), custom_call_target="tpu_custom_call" | custom-call | tf_op jit(solution)/shard_map/sparse_conv/pallas_call | solution.py:357
  94.5 0.0 copy-start
  94.6 2.1 %copy.13 = bf16[96,4096]{1,0:T(8,128)(2,1)} copy(bf16[96,4096]{1,0:T(8,128)(2,1)} %get-tuple-element.4) | data formatting | bytes 1572864
  96.7 0.0 copy-done
  96.7 0.7 copy.14
Async XLA Ops:
  94.5 2.1 %copy-start = (bf16[192,512]{1,0:T(8,128)(2,1)S(1)}, bf16[192,512]{1,0:T(8,128)(2,1)}, u32[]{:S(2)}) copy-start(bf16[192,512]{1,0:T(8,128)(2,1)} %get-tuple-element.5) | copy-start | bytes 589828

commit v5 on v4

--- a/solution.py
+++ b/solution.py
@@ -10,6 +10,7 @@
 LANES = 128
 QC = 1024
 STEP = 2
+WIDE = 2
 PARTS = 3
 MESH = pl.DeviceIdType.MESH
 
@@ -31,11 +32,14 @@
     hbm, refs = refs[:7], refs[7:]
     fine_ref, coarse_ref = refs[:2]
     here, in_sem = refs[2:9], refs[9]
-    compute(nx, ny, dest_ref, fine_ref, coarse_ref, hbm, here, in_sem, *refs[10:])
+    fine_here, fine_sem = refs[10:12]
+    fine_copy = pltpu.make_async_copy(fine_here, fine_ref, fine_sem)
+    compute(nx, ny, dest_ref, fine_here, coarse_ref, fine_copy, hbm, here, in_sem, *refs[12:])
+    fine_copy.wait()
 
 
 def compute(
-    nx, ny, dest_ref, fine_ref, coarse_ref, hbm, here, in_sem,
+    nx, ny, dest_ref, fine_ref, coarse_ref, fine_copy, hbm, here, in_sem,
     idx_a, idx_b, tiles, table, offered, halo, wpair, acc, part, out_x, in_x, out_y, in_y,
     idx_sem, halo_send, halo_recv, x_send, x_recv, y_send, y_recv,
     gain_ref, bias_ref,
@@ -181,6 +185,12 @@
             x = jnp.concatenate([halo[t, :, pl.ds(n * step, step)], pad], axis=0)
             table[pl.ds(slots + t * bnd + n * step, step), :] = dot_nt(ident, x)
 
+    for b in range(blocks):
+        own = [feat_ref[:, pl.ds(first_col(b, t), LANES)] for t in range(lane_tiles)]
+        acc[b] = jnp.dot(
+            w_ref[centre], jnp.concatenate(own, axis=1), preferred_element_type=F32
+        )
+
     tile_rows(4)
     for piece in range(PARTS):
         arrived(0, piece)
@@ -202,20 +212,23 @@
     def gather_multiply(t, s, e):
         b = lax.div(t, pairs)
         m = t - b * pairs
-        keep = jnp.where(m == 0, 0.0, 1.0)
         first = e * 2 * lane_tiles
-        for u in range(lane_tiles):
+        for u in range(0, lane_tiles, WIDE):
             sides = []
             for h in range(2):
-                at = [idx[s][first + h * lane_tiles + u, r] for r in range(LANES)]
+                at = [
+                    idx[s][first + h * lane_tiles + u + w, r]
+                    for w in range(WIDE)
+                    for r in range(LANES)
+                ]
                 eights = [
                     jnp.concatenate([table[pl.ds(a, 1), :] for a in at[r : r + 8]], axis=0)
-                    for r in range(0, LANES, 8)
+                    for r in range(0, WIDE * LANES, 8)
                 ]
                 sides.append(jnp.concatenate(eights, axis=0))
             g = jnp.concatenate(sides, axis=1).astype(BF16)
-            cols = slice(u * LANES, (u + 1) * LANES)
-            acc[b, :, cols] = acc[b, :, cols] * keep + dot_nt(wpair[m], g)
+            cols = slice(u * LANES, (u + WIDE) * LANES)
+            acc[b, :, cols] = acc[b, :, cols] + dot_nt(wpair[m], g)
 
     dest = dest_ref[0]
     out_x[:, pl.ds(out_channels, 16), :] = jnp.full(
@@ -252,9 +265,7 @@
             for u in range(lane_tiles):
                 p = half * lane_tiles + u
                 cols = pl.ds(pl.multiple_of(p * coarse_len + v * LANES, LANES), LANES)
-                conv = acc[b, :, u * LANES : (u + 1) * LANES] + jnp.dot(
-                    w_ref[centre], feat_ref[:, cols], preferred_element_type=F32
-                )
+                conv = acc[b, :, u * LANES : (u + 1) * LANES]
                 active = (map_ref[centre : centre + 1, cols] < slots).astype(F32)
                 fine = jnp.maximum(conv * gain_ref[...] + bias_ref[...], 0.0) * active
                 fine = fine.astype(BF16)
@@ -282,7 +293,6 @@
             to_down(v).start()
 
     part[...] = jnp.zeros_like(part)
-    acc[...] = jnp.zeros_like(acc)
     fetch(0, 0).start()
     fetch(1, 1).start()
 
@@ -311,6 +321,7 @@
     fetch(steps - 1, 0).wait()
     fetch(steps - 1, 1).wait()
 
+    fine_copy.start()
     onwards(chunks - 1)
     for v in range(chunks):
         @pl.when(has_up)
@@ -357,7 +368,7 @@
     fine, coarse = pl.pallas_call(
         kernel,
         in_specs=[smem] + [pl.BlockSpec(memory_space=pltpu.HBM)] * 7,
-        out_specs=[vmem] * 2,
+        out_specs=[pl.BlockSpec(memory_space=pltpu.HBM), vmem],
         out_shape=[
             jax.ShapeDtypeStruct((channels, slots), BF16),
             jax.ShapeDtypeStruct((out_channels, coarse_len), BF16),
@@ -371,6 +382,8 @@
             pltpu.VMEM((1, channels), F32),
             pltpu.VMEM(down_weight.shape, BF16),
             pltpu.SemaphoreType.DMA((7,)),
+            pltpu.VMEM(features.shape, BF16),
+            pltpu.SemaphoreType.DMA,
             pltpu.SMEM((STEP * 2 * QC // LANES, LANES), jnp.int32),
             pltpu.SMEM((STEP * 2 * QC // LANES, LANES), jnp.int32),
             pltpu.VMEM((total // STEP, STEP * 2 * QC // LANES, LANES), jnp.int32),

time: 97.5 us -> 96.3 us (0.988)
  Pallas kernels: 93.3 us -> 92 us
    pallas_call x1, Pallas kernels: 93.3 us -> 92 us  [shards(): pl.pallas_call(kernel, in_specs=[smem] + [pl.BlockSpec(memory_space=pltpu...]
where the time goes in v5:
time: 96.3 us; the launch traced here: 96.1 us
  Pallas kernels  92 us (96%)
  local copies, waits for them, and re-layouts  2.78 us (3%)
  between operations  1.3 us (1%)
    pallas_call x1, Pallas kernels, shards(): pl.pallas_call(kernel, in_specs=[smem] + [pl.BlockSpec(memory_space=pltpu...  92 us
    unnamed x4, local copies, waits for them, and re-layouts  2.78 us

profile of v5, /device:TPU:31, one launch (start us, length us, event | category | flops | bytes accessed | tf_op | source)
XLA Modules:
  0.0 96.1 jit_solution(6749795425624713701)
XLA Ops:
  1.3 92.0 %sparse_conv.1 = (bf16[96,4096]{1,0:T(8,128)(2,1)}, bf16[192,512]{1,0:T(8,128)(2,1)}) custom-call(s32[1]{0:T(128)S(6)} %copy.12.refs_0_, s32[1024]{0:T(1024)} %refs_1_.1, s32[27,4096]{1,0:T(8,128)} %refs_2_.1, bf16[96,4096]{1,0:T(8,128)(2,1)} %refs_3_.1, bf16[27,96,96]{2,1,0:T(8,128)(2,1)} %refs_4_.1, f32[1,96]{1,0:T(1,128)} %bitcast.2, f32[1,96]{1,0:T(1,128)} %bitcast.3, ...), custom_call_target="tpu_custom_call" | custom-call | tf_op jit(solution)/shard_map/sparse_conv/pallas_call | solution.py:368
  93.3 0.0 copy-start
  93.3 2.1 %copy.13 = bf16[96,4096]{1,0:T(8,128)(2,1)} copy(bf16[96,4096]{1,0:T(8,128)(2,1)} %get-tuple-element.4) | data formatting | bytes 1572864
  95.4 0.0 copy-done
  95.5 0.7 copy.14
Async XLA Ops:
  93.3 2.1 %copy-start = (bf16[192,512]{1,0:T(8,128)(2,1)S(1)}, bf16[192,512]{1,0:T(8,128)(2,1)}, u32[]{:S(2)}) copy-start(bf16[192,512]{1,0:T(8,128)(2,1)} %get-tuple-element.5) | copy-start | bytes 589828
